TPU v7x, 32 devices: a whole 2x2x4 slice. The times are simulated.
32 devices in a mesh: row: 4 (over z), col: 4 (over y, core), dp: 2 (over x).
Axes of the slice: x: 2, y: 2, z: 4, core: 2. Of those that a mesh axis runs over, the one named last changes fastest.
Arguments:
- grad_out: bfloat16 [2, 128, 8192], P('dp', 'row', 'col'), may hold values from -6 to 6
- gate_pre: bfloat16 [2, 128, 28672], P('dp', 'col', 'row'), may hold values from -6 to 6
- up_pre: bfloat16 [2, 128, 28672], P('dp', 'col', 'row'), may hold values from -6 to 6
- w_down: bfloat16 [28672, 8192], P('row', 'col'), may hold values from -0.046875 to 0.046875
- block_mask: int32 [224, 64], replicated, may hold values 0 or 1
Outputs:
- grad_gate: bfloat16 [2, 128, 28672], P('dp', 'col', 'row')
- grad_up: bfloat16 [2, 128, 28672], P('dp', 'col', 'row')
- grad_down: bfloat16 [28672, 8192], P('row', 'col')
All inputs are finite; a program needn't handle non-finite values.
Results may differ from a plain program's by a relative error of at most 0.019.
Values may be sent and summed in bfloat16 or wider, within the bound.
No kernel may reach another device: no remote copies, remote signals or barrier semaphores. Data moves between devices by JAX's collectives and lax.ppermute only.
A program may use at most 256 MiB of HBM per device.

v0:
```python
import jax
import jax.numpy as jnp
from jax import lax
from jax.sharding import PartitionSpec as P

BLOCK = 128


def local_keep(block_mask, row_start, col_start, rows, cols):
    row_block = (row_start + jnp.arange(rows, dtype=jnp.int32)) // BLOCK
    col_block = (col_start + jnp.arange(cols, dtype=jnp.int32)) // BLOCK
    row_pick = (
        row_block[:, None] == jnp.arange(block_mask.shape[0], dtype=jnp.int32)[None, :]
    ).astype(jnp.float32)
    col_pick = (
        jnp.arange(block_mask.shape[1], dtype=jnp.int32)[:, None] == col_block[None, :]
    ).astype(jnp.float32)
    picked = jnp.dot(row_pick, block_mask.astype(jnp.float32), precision=lax.Precision.HIGHEST)
    return jnp.dot(picked, col_pick, precision=lax.Precision.HIGHEST)


def local(grad_out, gate_pre, up_pre, w_down, block_mask):
    f_local, d_local = w_down.shape
    row_start = lax.axis_index("row") * f_local
    col_start = lax.axis_index("col") * d_local
    keep = local_keep(block_mask, row_start, col_start, f_local, d_local) > 0.5
    w_kept = jnp.where(keep, w_down, jnp.zeros_like(w_down))
    gate = gate_pre[0].astype(jnp.float32)
    up = up_pre[0].astype(jnp.float32)
    sig = jax.nn.sigmoid(gate)
    act = (gate * sig * up).astype(jnp.bfloat16)
    act_all = lax.all_gather(act, "col", axis=0, tiled=True)
    group_tokens = act_all.shape[0]
    act_src = act_all[None]
    own_group = 0
    grad_all = lax.all_gather(grad_out, "row", axis=1, tiled=True)
    own_piece = lax.dynamic_index_in_dim(grad_all, own_group, 0, keepdims=False)
    term = lax.dot_general(
        own_piece, w_kept, (((1,), (1,)), ((), ())), preferred_element_type=jnp.float32
    )
    partial_value = term
    weight_grad = lax.dot_general(
        act_src, grad_all, (((0, 1), (0, 1)), ((), ())), preferred_element_type=jnp.float32
    )
    partial_value, weight_grad = (partial_value, weight_grad)
    dact = lax.psum_scatter(
        partial_value.astype(jnp.bfloat16), "col", scatter_dimension=0, tiled=True
    ).astype(jnp.float32)
    grad_gate = (dact * up * sig * (1.0 + gate * (1.0 - sig))).astype(jnp.bfloat16)
    grad_up = (dact * gate * sig).astype(jnp.bfloat16)
    weight_grad = lax.psum(weight_grad.astype(jnp.bfloat16), "dp").astype(jnp.float32)
    scale = 1.0 / jnp.sqrt(jnp.float32(lax.axis_size("dp") * group_tokens))
    grad_down = jnp.where(keep, weight_grad * scale, jnp.zeros_like(weight_grad)).astype(
        jnp.bfloat16
    )
    return (grad_gate[None], grad_up[None], grad_down)


def solution(mesh):
    placed = (
        P("dp", "row", "col"),
        P("dp", "col", "row"),
        P("dp", "col", "row"),
        P("row", "col"),
        P(),
    )
    return jax.shard_map(
        local,
        mesh=mesh,
        in_specs=placed,
        out_specs=(P("dp", "col", "row"), P("dp", "col", "row"), P("row", "col")),
        check_vma=False,
    )
```

profile of v0, /device:TPU:0, one launch (start us, length us, event | category | flops | bytes accessed | tf_op | source)
XLA Modules:
  0.0 830.7 jit_solution(7339044232521490903)
XLA Ops:
  7.2 0.0 reduce-scatter.4.cloned.1.call-start
  7.3 17.6 %all_gather.6 = bf16[1,128,2048]{2,1,0:T(8,128)(2,1)S(1)} all-gather(bf16[1,32,2048]{2,1,0:T(8,128)(2,1)} %param.5), channel_id=1, replica_groups=mesh['row'=4,'col'=4,'dp'=2] {'row'}, dimensions={1}, use_global_device_ids=true | all-gather | bytes 655360 | tf_op jit(solution)/shard_map/all_gather | solution.py:36
  24.8 4.7 fusion.9
  29.5 30.8 %broadcast_compare_fusion = pred[7168,2048]{1,0:T(32,128)(4,1)} fusion(f32[7168,64]{0,1:T(8,128)S(1)} %fusion.9, s32[2048]{0:T(1024)S(1)} %add_select_fusion.1), kind=kOutput, calls=%fused_computation.3 | convolution fusion | flops 11289100288 | bytes 16523264 | tf_op jit(solution)/shard_map/dot_general | solution.py:19
  60.4 0.0 copy-start
  60.4 0.0 copy-start.1
  60.4 16.7 %fusion.6 = bf16[128,7168]{0,1:T(8,128)(2,1)S(1)} fusion(pred[7168,2048]{1,0:T(32,128)(4,1)} %broadcast_compare_fusion, bf16[7168,2048]{1,0:T(8,128)(2,1)} %param.8, bf16[1,128,2048]{2,1,0:T(8,128)(2,1)S(1)} %all_gather.6), kind=kOutput, calls=%fused_computation.7 | convolution fusion | flops 3773693952 | bytes 46399488 | tf_op jit(solution)/shard_map/dot_general | solution.py:38
  77.1 2.9 copy.23
  80.0 0.0 reduce-scatter.4.cloned.1.call-update
  80.0 0.0 all-gather.2.cloned.1.call-start
  80.0 31.7 %reduce-scatter.4.cloned.1.call-done = bf16[32,7168]{1,0:T(8,128)(2,1)} async-done(((bf16[128,7168]{1,0:T(8,128)(2,1)}), bf16[32,7168]{1,0:T(8,128)(2,1)}) %reduce-scatter.4.cloned.1.call-update) | async-done | bytes 458768 | tf_op jit(solution)/shard_map/reduce_scatter | solution.py:46
  111.7 0.0 copy-done
  111.7 0.0 copy-done.1
  111.7 2.6 fusion.14
  114.3 0.0 all-gather.2.cloned.1.call-update
  114.3 0.0 all-reduce.2.cloned.1.call-start
  114.4 21.2 %all-gather.2.cloned.1.call-done = bf16[128,7168]{1,0:T(8,128)(2,1)} async-done(((bf16[32,7168]{1,0:T(8,128)(2,1)}), bf16[128,7168]{1,0:T(8,128)(2,1)}) %all-gather.2.cloned.1.call-update) | async-done | bytes 1835024 | tf_op jit(solution)/shard_map/all_gather | solution.py:32
  135.6 15.8 %convolution_convert_fusion = bf16[7168,2048]{1,0:T(8,128)(2,1)} fusion(bf16[128,7168]{1,0:T(8,128)(2,1)} %all-gather.2.cloned.1.call-done, bf16[1,128,2048]{2,1,0:T(8,128)(2,1)S(1)} %all_gather.6), kind=kOutput, calls=%fused_computation.4 | convolution fusion | flops 3772776448 | bytes 31719424 | tf_op jit(solution)/shard_map/dot_general | solution.py:42
  151.4 0.0 all-reduce.2.cloned.1.call-update
  151.4 647.9 %all-reduce.2.cloned.1.call-done = bf16[7168,2048]{1,0:T(8,128)(2,1)} async-done(((bf16[7168,2048]{1,0:T(8,128)(2,1)}), bf16[7168,2048]{1,0:T(8,128)(2,1)}) %all-reduce.2.cloned.1.call-update) | async-done | bytes 29360144 | tf_op jit(solution)/shard_map/psum | solution.py:51
  799.3 24.8 %select_convert_fusion = bf16[7168,2048]{1,0:T(8,128)(2,1)} fusion(pred[7168,2048]{1,0:T(32,128)(4,1)} %broadcast_compare_fusion, bf16[7168,2048]{1,0:T(8,128)(2,1)} %all-reduce.2.cloned.1.call-done), kind=kLoop, calls=%fused_computation | loop fusion | flops 58720256 | bytes 73400320 | tf_op jit(solution)/shard_map/convert_element_type | solution.py:53
  (2 shorter events, 0.0 us)
Async XLA Ops:
  7.2 104.5 %reduce-scatter.4.cloned.1.call-start = ((), (), s32[]{:S(2)}) async-start(), calls=%async_computation.3 | async-start | bytes 2293760 | tf_op jit(solution)/shard_map/reduce_scatter | solution.py:46
  60.4 51.3 %copy-start = (bf16[1,32,7168]{2,1,0:T(8,128)(2,1)S(1)}, bf16[1,32,7168]{2,1,0:T(8,128)(2,1)}, u32[]{:S(2)}) copy-start(bf16[1,32,7168]{2,1,0:T(8,128)(2,1)} %param.7) | copy-start | bytes 1376260
  60.4 51.3 %copy-start.1 = (bf16[1,32,7168]{2,1,0:T(8,128)(2,1)S(1)}, bf16[1,32,7168]{2,1,0:T(8,128)(2,1)}, u32[]{:S(2)}) copy-start(bf16[1,32,7168]{2,1,0:T(8,128)(2,1)} %param.6) | copy-start | bytes 1376260
  80.0 55.6 %all-gather.2.cloned.1.call-start = ((), (), s32[]{:S(2)}) async-start(), calls=%async_computation.1 | async-start | bytes 2293760 | tf_op jit(solution)/shard_map/all_gather | solution.py:32
  114.3 685.0 %all-reduce.2.cloned.1.call-start = ((), (), s32[]{:S(2)}) async-start(), calls=%async_computation.2 | async-start | bytes 58720256 | tf_op jit(solution)/shard_map/psum | solution.py:51
Sparse Core Ops, SparseCore 0:
  80.1 31.5 reduce-scatter.3
  114.4 21.1 all-gather.1
  151.6 647.7 all-reduce.1
where the time goes:
time: 831 us
  waiting for transfers between devices  701 us (84%)
  matrix products  68 us (8%)
  other arithmetic  27.4 us (3%)
  blocking collectives  17.6 us (2%)
  between operations  13.8 us (2%)
    psum x1, waiting for transfers between devices, local(): lax.psum(weight_grad.astype(jnp.bfloat16), 'dp').astype(jnp.float32)  648 us
    reduce_scatter x1, waiting for transfers between devices, local(): lax.psum_scatter(partial_value.astype(jnp.bfloat16), 'col', scatter_dimen...  31.7 us
    dot_general x1, matrix products, local_keep(): return jnp.dot(picked, col_pick, precision=lax.Precision.HIGHEST)  30.8 us
    convert_element_type x1, other arithmetic, local(): jnp.where(keep, weight_grad * scale, jnp.zeros_like(weight_grad))  24.8 us
    all_gather x1, waiting for transfers between devices, local(): act_all = lax.all_gather(act, 'col', axis=0, tiled=True)  21.2 us
    all_gather x1, blocking collectives, local(): grad_all = lax.all_gather(grad_out, 'row', axis=1, tiled=True)  17.6 us
    dot_general x1, matrix products, local(): lax.dot_general(own_piece, w_kept, (((1,), (1,)), ((), ())), preferred_el...  16.7 us
  transfers between devices with their start and end apart: 3, of which 3 were waited for; matrix products, arithmetic and copies ran while one was open for 0% of the time, Pallas kernels for 0%

commit v1 on v0

v1 whole, which is shorter than its diff:
```python
import functools

import jax
import jax.numpy as jnp
from jax import lax
from jax.experimental import pallas as pl
from jax.experimental.pallas import tpu as pltpu
from jax.sharding import PartitionSpec as P

BLOCK = 128
ACT_CHUNKS = 2
SUM_CHUNKS = 2
VMEM_LIMIT = 40 * 1024 * 1024
bf16 = jnp.bfloat16
f32 = jnp.float32


def tile_of(size, largest):
    tile = largest
    while size % tile:
        tile //= 2
    return tile


def swap(x, axis, bit):
    n = lax.axis_size(axis)
    return lax.ppermute(x, axis, [(i, i ^ bit) for i in range(n)])


def masked_rows(w, mask_rows):
    parts = [
        w[k * BLOCK : (k + 1) * BLOCK, :] * m.astype(bf16) for k, m in enumerate(mask_rows)
    ]
    return parts[0] if len(parts) == 1 else jnp.concatenate(parts, axis=0)


def partial_kernel(base, place_ref, g0, g1, g2, g3, mask_ref, w_ref, stay_ref, next_ref, send_ref, lhs):
    step = pl.program_id(0)
    rows = g0.shape[0]

    @pl.when(step == 0)
    def _():
        for s, g in enumerate((g0, g1, g2, g3)):
            at = pl.multiple_of(place_ref[s] * rows, rows)
            lhs[pl.ds(at, rows), :] = g[...]

    tile = w_ref.shape[0]
    sub = min(tile, 256)
    for k in range(tile // sub):
        block = base + step * (tile // BLOCK) + k * (sub // BLOCK)
        masks = [mask_ref[pl.ds(block + j, 1), :] for j in range(sub // BLOCK)]
        w = masked_rows(w_ref[k * sub : (k + 1) * sub, :], masks)
        out = lax.dot_general(
            lhs[...], w, (((1,), (1,)), ((), ())), preferred_element_type=f32
        ).astype(bf16)
        at = slice(k * sub, (k + 1) * sub)
        stay_ref[:, at] = out[:rows]
        next_ref[:, at] = out[rows : 2 * rows]
        send_ref[:, at] = out[2 * rows :]


def partial_sums(place, grads, mask_rows, w, start, width):
    f_local, d_local = w.shape
    rows = grads[0].shape[0]
    tile = tile_of(width, 512)
    base = start // BLOCK
    whole = pl.BlockSpec((rows, d_local), lambda i, p: (0, 0))
    return pl.pallas_call(
        functools.partial(partial_kernel, base),
        grid_spec=pltpu.PrefetchScalarGridSpec(
            num_scalar_prefetch=1,
            grid=(width // tile,),
            in_specs=[whole] * 4
            + [
                pl.BlockSpec(mask_rows.shape, lambda i, p: (0, 0)),
                pl.BlockSpec((tile, d_local), lambda i, p: (start // tile + i, 0)),
            ],
            out_specs=[
                pl.BlockSpec((rows, tile), lambda i, p: (0, i)),
                pl.BlockSpec((rows, tile), lambda i, p: (0, i)),
                pl.BlockSpec((2 * rows, tile), lambda i, p: (0, i)),
            ],
            scratch_shapes=[pltpu.VMEM((4 * rows, d_local), bf16)],
        ),
        out_shape=[
            jax.ShapeDtypeStruct((rows, width), bf16),
            jax.ShapeDtypeStruct((rows, width), bf16),
            jax.ShapeDtypeStruct((2 * rows, width), bf16),
        ],
        compiler_params=pltpu.CompilerParams(vmem_limit_bytes=VMEM_LIMIT),
        cost_estimate=pl.CostEstimate(
            flops=2 * 4 * rows * width * d_local, bytes_accessed=2 * width * d_local, transcendentals=0
        ),
        name="partial_sums",
    )(place, *grads, mask_rows, w)


def weight_kernel(base, aliased, place_ref, *refs):
    acts, grads = refs[:8], refs[8:16]
    mask_ref = refs[16]
    out_ref, lhs, rhs = refs[17 + aliased :]
    step = pl.program_id(0)
    rows = grads[0].shape[0]

    @pl.when(step == 0)
    def _():
        for s, g in enumerate(grads):
            at = pl.multiple_of(place_ref[s] * rows, rows)
            rhs[pl.ds(at, rows), :] = g[...]

    for s, a in enumerate(acts):
        lhs[s * rows : (s + 1) * rows, :] = a[...]
    tile, d_local = out_ref.shape
    total = lax.dot_general(
        lhs[...], rhs[...], (((0,), (0,)), ((), ())), preferred_element_type=f32
    )
    for k in range(tile // BLOCK):
        m = mask_ref[pl.ds(base + step * (tile // BLOCK) + k, 1), :]
        at = slice(k * BLOCK, (k + 1) * BLOCK)
        out_ref[at, :] = (total[at, :] * m).astype(bf16)


def weight_grad(place, acts, grads, mask_scaled, start, f_local, so_far):
    rows, width = acts[0].shape
    d_local = grads[0].shape[1]
    tile = tile_of(width, 512)
    aliased = 0 if so_far is None else 1
    in_specs = (
        [pl.BlockSpec((rows, tile), lambda i, p: (0, i))] * 8
        + [pl.BlockSpec((rows, d_local), lambda i, p: (0, 0))] * 8
        + [pl.BlockSpec(mask_scaled.shape, lambda i, p: (0, 0))]
        + [pl.BlockSpec(memory_space=pl.ANY)] * aliased
    )
    operands = (place, *acts, *grads, mask_scaled) + ((so_far,) if aliased else ())
    return pl.pallas_call(
        functools.partial(weight_kernel, start // BLOCK, aliased),
        grid_spec=pltpu.PrefetchScalarGridSpec(
            num_scalar_prefetch=1,
            grid=(width // tile,),
            in_specs=in_specs,
            out_specs=pl.BlockSpec((tile, d_local), lambda i, p: (start // tile + i, 0)),
            scratch_shapes=[
                pltpu.VMEM((8 * rows, tile), bf16),
                pltpu.VMEM((8 * rows, d_local), bf16),
            ],
        ),
        out_shape=jax.ShapeDtypeStruct((f_local, d_local), bf16),
        input_output_aliases={18: 0} if aliased else {},
        compiler_params=pltpu.CompilerParams(vmem_limit_bytes=VMEM_LIMIT),
        cost_estimate=pl.CostEstimate(
            flops=2 * 8 * rows * width * d_local, bytes_accessed=2 * width * d_local, transcendentals=0
        ),
        name="weight_grad",
    )(*operands)


def activation(gate, up):
    gate, up = gate.astype(f32), up.astype(f32)
    return (gate * jax.nn.sigmoid(gate) * up).astype(bf16)


def local(grad_out, gate_pre, up_pre, w_down, block_mask):
    f_local, d_local = w_down.shape
    row, col = lax.axis_index("row"), lax.axis_index("col")
    scale = 1.0 / jnp.sqrt(f32(lax.axis_size("dp") * lax.axis_size("row") * grad_out.shape[1]))
    own_mask = lax.dynamic_slice(
        block_mask,
        (row * (f_local // BLOCK), col * (d_local // BLOCK)),
        (f_local // BLOCK, d_local // BLOCK),
    )
    keep = jnp.repeat((own_mask > 0).astype(f32), BLOCK, axis=1)
    keep_scaled = keep * scale

    own = grad_out[0]
    rows = own.shape[0]
    grads = [own] + [swap(own, "row", s) for s in (1, 2, 3)]
    across = swap(own, "dp", 1)

    gate, up = gate_pre[0], up_pre[0]
    width = f_local // ACT_CHUNKS
    act_pieces = []
    for j in range(ACT_CHUNKS):
        at = slice(j * width, (j + 1) * width)
        a = activation(gate[:, at], up[:, at])
        a_y = swap(a, "col", 2)
        a_x = swap(a, "dp", 1)
        a_xy = swap(a_y, "dp", 1)
        act_pieces.append(
            [
                a, swap(a, "col", 1), a_y, swap(a_y, "col", 1),
                a_x, swap(a_x, "col", 1), a_xy, swap(a_xy, "col", 1),
            ]
        )
    others = [across] + [swap(across, "row", s) for s in (1, 2, 3)]

    away = jnp.stack([row ^ col ^ s for s in range(4)]).astype(jnp.int32)
    by_dest = jnp.array([0, 2, 1, 3], jnp.int32)[away]
    by_act = jnp.concatenate([away, away + 4])

    span = f_local // SUM_CHUNKS
    sums = []
    for j in range(SUM_CHUNKS):
        stay, onward, send = partial_sums(by_dest, grads, keep, w_down, j * span, span)
        got = swap(send, "col", 1)
        mine = stay.astype(f32) + got[:rows].astype(f32)
        theirs = (onward.astype(f32) + got[rows:].astype(f32)).astype(bf16)
        sums.append((mine, swap(theirs, "col", 2)))

    grad_down = None
    for j in range(ACT_CHUNKS):
        grad_down = weight_grad(
            by_act, act_pieces[j], grads + others, keep_scaled, j * width, f_local, grad_down
        )

    gg, gu = [], []
    for j, (mine, got) in enumerate(sums):
        at = slice(j * span, (j + 1) * span)
        dact = mine + got.astype(f32)
        g, u = gate[:, at].astype(f32), up[:, at].astype(f32)
        sig = jax.nn.sigmoid(g)
        gg.append((dact * u * sig * (1.0 + g * (1.0 - sig))).astype(bf16))
        gu.append((dact * g * sig).astype(bf16))
    return (
        jnp.concatenate(gg, axis=1)[None],
        jnp.concatenate(gu, axis=1)[None],
        grad_down,
    )


def general(grad_out, gate_pre, up_pre, w_down, block_mask):
    f_local, d_local = w_down.shape
    row_block = (lax.axis_index("row") * f_local + jnp.arange(f_local)) // BLOCK
    col_block = (lax.axis_index("col") * d_local + jnp.arange(d_local)) // BLOCK
    keep = block_mask[row_block][:, col_block] > 0
    w_kept = jnp.where(keep, w_down, jnp.zeros_like(w_down))
    gate, up = gate_pre[0].astype(f32), up_pre[0].astype(f32)
    sig = jax.nn.sigmoid(gate)
    act = (gate * sig * up).astype(bf16)
    grads = lax.all_gather(grad_out[0], "row", axis=0, tiled=True)
    partial = lax.dot_general(
        grads, w_kept, (((1,), (1,)), ((), ())), preferred_element_type=f32
    ).astype(bf16)
    dact = lax.psum_scatter(partial, "col", scatter_dimension=0, tiled=True).astype(f32)
    acts = lax.all_gather(act, ("dp", "col"), axis=0, tiled=True)
    every = lax.all_gather(grads, "dp", axis=0, tiled=True)
    total = lax.dot_general(acts, every, (((0,), (0,)), ((), ())), preferred_element_type=f32)
    scale = 1.0 / jnp.sqrt(f32(every.shape[0]))
    grad_down = jnp.where(keep, total * scale, jnp.zeros_like(total)).astype(bf16)
    grad_gate = (dact * up * sig * (1.0 + gate * (1.0 - sig))).astype(bf16)
    grad_up = (dact * gate * sig).astype(bf16)
    return grad_gate[None], grad_up[None], grad_down


def solution(mesh):
    placed = (
        P("dp", "row", "col"),
        P("dp", "col", "row"),
        P("dp", "col", "row"),
        P("row", "col"),
        P(),
    )
    size = dict(mesh.shape)
    pairwise = size["row"] == 4 and size["col"] == 4 and size["dp"] == 2

    def run(grad_out, gate_pre, up_pre, w_down, block_mask):
        f_local, d_local = w_down.shape
        rows = grad_out.shape[1]
        fits = pairwise and rows == gate_pre.shape[1] and rows % 16 == 0
        for chunks in (ACT_CHUNKS, SUM_CHUNKS):
            fits = fits and f_local % (chunks * BLOCK) == 0
        fits = fits and d_local % BLOCK == 0
        step = local if fits else general
        return step(grad_out, gate_pre, up_pre, w_down, block_mask)

    return jax.shard_map(
        run,
        mesh=mesh,
        in_specs=placed,
        out_specs=(P("dp", "col", "row"), P("dp", "col", "row"), P("row", "col")),
        check_vma=False,
    )
```

time: 831 us -> 103 us (0.12)
  waiting for transfers between devices: 701 us -> 31.5 us
  matrix products: 68 us -> 0 us
  Pallas kernels: 0 us -> 39.2 us
  starting transfers between devices: 0.12 us -> 23.4 us
  other arithmetic: 27.4 us -> 4.81 us
  blocking collectives: 17.6 us -> 0 us
  between operations: 13.8 us -> 0.74 us
    psum x1 -> x0, waiting for transfers between devices: 648 us -> none  [local(): lax.psum(weight_grad.astype(jnp.bfloat16), 'dp').astype(jnp.float32)]
    dot_general x4 -> x0, matrix products: 68 us -> none  [the longest x1 30.8 us: local_keep(): return jnp.dot(picked, col_pick, precision=lax.Precision.HIGHEST)]
    pallas_call x0 -> x4, Pallas kernels: none -> 39.2 us  [the longest x2 21 us: partial_sums(): pl.pallas_call(functools.partial(partial_kernel, base), grid_spec=pltpu.P...]
    reduce_scatter x1 -> x0, waiting for transfers between devices: 31.7 us -> none  [local(): lax.psum_scatter(partial_value.astype(jnp.bfloat16), 'col', scatter_dimen...]
    ppermute x0 -> x25, waiting for transfers between devices: none -> 31.5 us  [swap(): return lax.ppermute(x, axis, [(i, i ^ bit) for i in range(n)])]
    convert_element_type x2 -> x4, other arithmetic: 27.4 us -> 2.34 us  [the longest x1 1.44 us: local(): gu.append((dact * g * sig).astype(bf16))]
    ppermute x0 -> x25, starting transfers between devices: none -> 23.4 us  [swap(): return lax.ppermute(x, axis, [(i, i ^ bit) for i in range(n)])]
    all_gather x1 -> x0, waiting for transfers between devices: 21.2 us -> none  [local(): act_all = lax.all_gather(act, 'col', axis=0, tiled=True)]
  transfers between devices with their start and end apart: 3 -> 25, of which waited for: 3 -> 10; matrix products, arithmetic and copies ran while one was open for 0% -> 6% of each run, Pallas kernels for 0% -> 19%
where the time goes in v1:
time: 103 us
  Pallas kernels  39.2 us (38%)
  waiting for transfers between devices  31.5 us (31%)
  starting transfers between devices  23.4 us (23%)
  other arithmetic  4.81 us (5%)
  local copies, waits for them, and re-layouts  3.31 us (3%)
    ppermute x25, waiting for transfers between devices, swap(): return lax.ppermute(x, axis, [(i, i ^ bit) for i in range(n)])  31.5 us
    ppermute x25, starting transfers between devices, swap(): return lax.ppermute(x, axis, [(i, i ^ bit) for i in range(n)])  23.4 us
    pallas_call x2, Pallas kernels, partial_sums(): pl.pallas_call(functools.partial(partial_kernel, base), grid_spec=pltpu.P...  21 us
    pallas_call x2, Pallas kernels, weight_grad(): pl.pallas_call(functools.partial(weight_kernel, start // BLOCK, aliased),...  18.2 us
    broadcast_in_dim x1, other arithmetic, local(): jnp.concatenate(gg, axis=1)[None]  2.14 us
  transfers between devices with their start and end apart: 25, of which 10 were waited for; matrix products, arithmetic and copies ran while one was open for 6% of the time, Pallas kernels for 19%

profile of v1, /device:TPU:0, one launch (start us, length us, event | category | flops | bytes accessed | tf_op | source)
XLA Modules:
  0.0 102.9 jit_solution(8534992962549342699)
XLA Ops:
  0.6 5.1 %collective-permute-start.2 = (bf16[32,2048]{1,0:T(8,128)(2,1)}, bf16[32,2048]{1,0:T(8,128)(2,1)S(1)}, u32[]{:S(2)}, u32[]{:S(2)}) collective-permute-start(bf16[32,2048]{1,0:T(8,128)(2,1)} %bitcast.25), channel_id=1, source_target_pairs={{0,24},{8,16},{16,8},{24,0},{1,25},{9,17},{17,9},{25,1},{2,26},{10... | collective-permute-start | bytes 393224 | tf_op jit(solution)/shard_map/ppermute | solution.py:27
  10.4 6.6 %collective-permute-done.1.g2.refs_10_ = bf16[32,2048]{1,0:T(8,128)(2,1)S(1)} collective-permute-done((bf16[32,2048]{1,0:T(8,128)(2,1)}, bf16[32,2048]{1,0:T(8,128)(2,1)S(1)}, u32[]{:S(2)}, u32[]{:S(2)}) %collective-permute-start.1) | collective-permute-done | bytes 131104 | tf_op jit(solution)/shard_map/ppermute | solution.py:27
  17.9 10.5 %partial_sums.2 = (bf16[32,3584]{1,0:T(8,128)(2,1)S(1)}, bf16[32,3584]{1,0:T(8,128)(2,1)S(1)}, bf16[64,3584]{1,0:T(8,128)(2,1)S(1)}) custom-call(s32[4]{0:T(128)S(1)} %gather_fusion, bf16[32,2048]{1,0:T(8,128)(2,1)S(1)} %bitcast.28, bf16[32,2048]{1,0:T(8,128)(2,1)S(1)} %collective-permute-done.g1.refs_9_, ...), custom_call_target="tpu_custom_call" | custom-call | flops 1879048192 | bytes 14680064 | tf_op jit(solution)/shard_map/partial_sums/pallas_call | solution.py:68
  28.5 10.5 %partial_sums.3 = (bf16[32,3584]{1,0:T(8,128)(2,1)S(1)}, bf16[32,3584]{1,0:T(8,128)(2,1)S(1)}, bf16[64,3584]{1,0:T(8,128)(2,1)S(1)}) custom-call(s32[4]{0:T(128)S(1)} %gather_fusion, bf16[32,2048]{1,0:T(8,128)(2,1)S(1)} %bitcast.29, bf16[32,2048]{1,0:T(8,128)(2,1)S(1)} %collective-permute-done.g1.refs_9_, ...), custom_call_target="tpu_custom_call" | custom-call | flops 1879048192 | bytes 14680064 | tf_op jit(solution)/shard_map/partial_sums/pallas_call | solution.py:68
  39.7 1.6 %collective-permute-start.4 = (bf16[32,3584]{1,0:T(8,128)(2,1)S(1)}, bf16[32,3584]{1,0:T(8,128)(2,1)S(1)}, u32[]{:S(2)}, u32[]{:S(2)}) collective-permute-start(bf16[32,3584]{1,0:T(8,128)(2,1)S(1)} %add_convert_fusion.1), channel_id=1, source_target_pairs={{0,4},{2,6},{4,0},{6,2},{1,5},{3,7},{5,1},{7,3},{8,12},{10,14},{12... | collective-permute-start | bytes 688136 | tf_op jit(solution)/shard_map/ppermute | solution.py:27
  41.3 1.4 %collective-permute-start.6 = (bf16[32,3584]{1,0:T(8,128)(2,1)S(1)}, bf16[32,3584]{1,0:T(8,128)(2,1)S(1)}, u32[]{:S(2)}, u32[]{:S(2)}) collective-permute-start(bf16[32,3584]{1,0:T(8,128)(2,1)S(1)} %add_convert_fusion), channel_id=1, source_target_pairs={{0,4},{2,6},{4,0},{6,2},{1,5},{3,7},{5,1},{7,3},{8,12},{10,14},{12... | collective-permute-start | bytes 688136 | tf_op jit(solution)/shard_map/ppermute | solution.py:27
  42.7 1.5 %collective-permute-start.14 = (bf16[32,2048]{1,0:T(8,128)(2,1)S(1)}, bf16[32,2048]{1,0:T(8,128)(2,1)S(1)}, u32[]{:S(2)}, u32[]{:S(2)}) collective-permute-start(bf16[32,2048]{1,0:T(8,128)(2,1)S(1)} %bitcast.30), channel_id=1, source_target_pairs={{0,1},{1,0},{2,3},{3,2},{4,5},{5,4},{6,7},{7,6},{8,9},{9,8},{10,11... | collective-permute-start | bytes 393224 | tf_op jit(solution)/shard_map/ppermute | solution.py:27
  44.2 4.0 %collective-permute-done.4 = bf16[32,3584]{1,0:T(8,128)(2,1)S(1)} collective-permute-done((bf16[32,3584]{1,0:T(8,128)(2,1)S(1)}, bf16[32,3584]{1,0:T(8,128)(2,1)S(1)}, u32[]{:S(2)}, u32[]{:S(2)}) %collective-permute-start.4) | collective-permute-done | bytes 229408 | tf_op jit(solution)/shard_map/ppermute | solution.py:27
  48.2 4.0 %collective-permute-done.6 = bf16[32,3584]{1,0:T(8,128)(2,1)S(1)} collective-permute-done((bf16[32,3584]{1,0:T(8,128)(2,1)S(1)}, bf16[32,3584]{1,0:T(8,128)(2,1)S(1)}, u32[]{:S(2)}, u32[]{:S(2)}) %collective-permute-start.6) | collective-permute-done | bytes 229408 | tf_op jit(solution)/shard_map/ppermute | solution.py:27
  52.2 1.4 %fusion.19 = (bf16[32,3584]{1,0:T(8,128)(2,1)S(1)}, bf16[32,3584]{1,0:T(8,128)(2,1)}, bf16[32,3584]{1,0:T(8,128)(2,1)S(1)}, bf16[32,3584]{1,0:T(8,128)(2,1)S(1)}...) fusion(bf16[32,3584]{1,0:T(8,128)(2,1)S(1)} %collective-permute-done.6, bf16[32,3584]{1,0:T(8,128)(2,1)S(1)} %get-tuple-element.12, ...), kind=kLoop, calls=%fused_computation.32 | loop fusion | flops 5275648 | bytes 3670016 | tf_op jit(solution)/shard_map/convert_element_type | solution.py:222
  53.6 1.5 %collective-permute-start.19 = (bf16[32,3584]{1,0:T(8,128)(2,1)S(1)}, bf16[32,3584]{1,0:T(8,128)(2,1)S(1)}, u32[]{:S(2)}, u32[]{:S(2)}) collective-permute-start(bf16[32,3584]{1,0:T(8,128)(2,1)S(1)} %get-tuple-element.19.refs_0_), channel_id=1, source_target_pairs={{0,4},{2,6},{4,0},{6,2},{1,5},{3,7},{5,1},{7,3},{8,12},{10,14},{12... | collective-permute-start | bytes 688136 | tf_op jit(solution)/shard_map/ppermute | solution.py:27
  55.2 2.5 %collective-permute-start.17 = (bf16[32,2048]{1,0:T(8,128)(2,1)S(1)}, bf16[32,2048]{1,0:T(8,128)(2,1)S(1)}, u32[]{:S(2)}, u32[]{:S(2)}) collective-permute-start(bf16[32,2048]{1,0:T(8,128)(2,1)S(1)} %collective-permute-done.14.refs_12_), channel_id=1, source_target_pairs={{0,24},{8,16},{16,8},{24,0},{1,25},{9,17},{17,9},{25,1},{2,26},{10... | collective-permute-start | bytes 393224 | tf_op jit(solution)/shard_map/ppermute | solution.py:27
  57.6 1.9 %collective-permute-start.15 = (bf16[32,2048]{1,0:T(8,128)(2,1)S(1)}, bf16[32,2048]{1,0:T(8,128)(2,1)S(1)}, u32[]{:S(2)}, u32[]{:S(2)}) collective-permute-start(bf16[32,2048]{1,0:T(8,128)(2,1)S(1)} %collective-permute-done.14.refs_12_), channel_id=1, source_target_pairs={{0,8},{8,0},{16,24},{24,16},{1,9},{9,1},{17,25},{25,17},{2,10},{10... | collective-permute-start | bytes 393224 | tf_op jit(solution)/shard_map/ppermute | solution.py:27
  59.5 1.5 %collective-permute-start.21 = (bf16[32,3584]{1,0:T(8,128)(2,1)S(1)}, bf16[32,3584]{1,0:T(8,128)(2,1)S(1)}, u32[]{:S(2)}, u32[]{:S(2)}) collective-permute-start(bf16[32,3584]{1,0:T(8,128)(2,1)S(1)} %get-tuple-element.19.refs_0_), channel_id=1, source_target_pairs={{0,1},{1,0},{2,3},{3,2},{4,5},{5,4},{6,7},{7,6},{8,9},{9,8},{10,11... | collective-permute-start | bytes 688136 | tf_op jit(solution)/shard_map/ppermute | solution.py:27
  61.0 2.4 %collective-permute-done.17.refs_15_ = bf16[32,2048]{1,0:T(8,128)(2,1)S(1)} collective-permute-done((bf16[32,2048]{1,0:T(8,128)(2,1)S(1)}, bf16[32,2048]{1,0:T(8,128)(2,1)S(1)}, u32[]{:S(2)}, u32[]{:S(2)}) %collective-permute-start.17) | collective-permute-done | bytes 131104 | tf_op jit(solution)/shard_map/ppermute | solution.py:27
  63.4 4.4 %collective-permute-done.16.refs_14_ = bf16[32,2048]{1,0:T(8,128)(2,1)S(1)} collective-permute-done((bf16[32,2048]{1,0:T(8,128)(2,1)S(1)}, bf16[32,2048]{1,0:T(8,128)(2,1)S(1)}, u32[]{:S(2)}, u32[]{:S(2)}) %collective-permute-start.16) | collective-permute-done | bytes 131104 | tf_op jit(solution)/shard_map/ppermute | solution.py:27
  68.3 1.5 %collective-permute-start.23 = (bf16[32,3584]{1,0:T(8,128)(2,1)S(1)}, bf16[32,3584]{1,0:T(8,128)(2,1)S(1)}, u32[]{:S(2)}, u32[]{:S(2)}) collective-permute-start(bf16[32,3584]{1,0:T(8,128)(2,1)S(1)} %collective-permute-done.19.refs_2_), channel_id=1, source_target_pairs={{0,1},{1,0},{2,3},{3,2},{4,5},{5,4},{6,7},{7,6},{8,9},{9,8},{10,11... | collective-permute-start | bytes 688136 | tf_op jit(solution)/shard_map/ppermute | solution.py:27
  71.2 3.5 %collective-permute-done.8.refs_2_ = bf16[32,3584]{1,0:T(8,128)(2,1)S(1)} collective-permute-done((bf16[32,3584]{1,0:T(8,128)(2,1)S(1)}, bf16[32,3584]{1,0:T(8,128)(2,1)S(1)}, u32[]{:S(2)}, u32[]{:S(2)}) %collective-permute-start.8) | collective-permute-done | bytes 229408 | tf_op jit(solution)/shard_map/ppermute | solution.py:27
  74.7 1.5 %collective-permute-start.12 = (bf16[32,3584]{1,0:T(8,128)(2,1)S(1)}, bf16[32,3584]{1,0:T(8,128)(2,1)S(1)}, u32[]{:S(2)}, u32[]{:S(2)}) collective-permute-start(bf16[32,3584]{1,0:T(8,128)(2,1)S(1)} %collective-permute-done.8.refs_2_), channel_id=1, source_target_pairs={{0,1},{1,0},{2,3},{3,2},{4,5},{5,4},{6,7},{7,6},{8,9},{9,8},{10,11... | collective-permute-start | bytes 688136 | tf_op jit(solution)/shard_map/ppermute | solution.py:27
  76.9 2.1 %maximum_bitcast_fusion = (bf16[1,32,7168]{2,1,0:T(8,128)(2,1)}, bf16[1,32,7168]{2,1,0:T(8,128)(2,1)}) fusion(bf16[32,3584]{1,0:T(8,128)(2,1)} %get-tuple-element.18, bf16[32,3584]{1,0:T(8,128)(2,1)} %get-tuple-element.21, bf16[32,3584]{1,0:T(8,128)(2,1)S(1)} %get-tuple-element.17, bf16[32,3584]{1,0:T(8,128)(2,1)} %get-tuple-element.22), kind=kLoop, calls=%fused_computation.34 | loop fusion | flops 1835008 | bytes 1835008 | tf_op jit(solution)/shard_map/broadcast_in_dim | solution.py:224
  79.0 2.8 %collective-permute-done.10.refs_4_ = bf16[32,3584]{1,0:T(8,128)(2,1)S(1)} collective-permute-done((bf16[32,3584]{1,0:T(8,128)(2,1)S(1)}, bf16[32,3584]{1,0:T(8,128)(2,1)S(1)}, u32[]{:S(2)}, u32[]{:S(2)}) %collective-permute-start.10) | collective-permute-done | bytes 229408 | tf_op jit(solution)/shard_map/ppermute | solution.py:27
  82.4 2.4 %collective-permute-done.12.refs_6_ = bf16[32,3584]{1,0:T(8,128)(2,1)S(1)} collective-permute-done((bf16[32,3584]{1,0:T(8,128)(2,1)S(1)}, bf16[32,3584]{1,0:T(8,128)(2,1)S(1)}, u32[]{:S(2)}, u32[]{:S(2)}) %collective-permute-start.12) | collective-permute-done | bytes 229408 | tf_op jit(solution)/shard_map/ppermute | solution.py:27
  84.7 9.1 %weight_grad.2.refs_17_ = bf16[7168,2048]{1,0:T(8,128)(2,1)} custom-call(s32[8]{0:T(128)S(1)} %concatenate.31.place_ref, bf16[32,3584]{1,0:T(8,128)(2,1)S(1)} %get-tuple-element.19.refs_0_, bf16[32,3584]{1,0:T(8,128)(2,1)S(1)} %collective-permute-done.18.refs_1_, bf16[32,3584]{1,0:T(8,128)(2,1)S(1)} %collective-permute-done.19.refs_2_, ...), custom_call_target="tpu_custom_call" | custom-call | flops 3758096384 | bytes 14680064 | tf_op jit(solution)/shard_map/weight_grad/pallas_call | solution.py:135
  93.8 9.1 %weight_grad.3 = bf16[7168,2048]{1,0:T(8,128)(2,1)} custom-call(s32[8]{0:T(128)S(1)} %concatenate.31.place_ref, bf16[32,3584]{1,0:T(8,128)(2,1)S(1)} %get-tuple-element.20.refs_0_, bf16[32,3584]{1,0:T(8,128)(2,1)S(1)} %collective-permute-done.7.refs_1_, bf16[32,3584]{1,0:T(8,128)(2,1)S(1)} %collective-permute-done.8.refs_2_, ...), custom_call_target="tpu_custom_call", output_to_operand_aliasing={{}: (18, {})} | custom-call | flops 3758096384 | bytes 14680064 | tf_op jit(solution)/shard_map/weight_grad/pallas_call | solution.py:135
  (56 shorter events, 9.5 us)
Async XLA Ops:
  0.6 9.8 %collective-permute-start.2 = (bf16[32,2048]{1,0:T(8,128)(2,1)}, bf16[32,2048]{1,0:T(8,128)(2,1)S(1)}, u32[]{:S(2)}, u32[]{:S(2)}) collective-permute-start(bf16[32,2048]{1,0:T(8,128)(2,1)} %bitcast.25), channel_id=1, source_target_pairs={{0,24},{8,16},{16,8},{24,0},{1,25},{9,17},{17,9},{25,1},{2,26},{10... | collective-permute-start | bytes 393224 | tf_op jit(solution)/shard_map/ppermute | solution.py:27
  5.7 11.3 %collective-permute-start.1 = (bf16[32,2048]{1,0:T(8,128)(2,1)}, bf16[32,2048]{1,0:T(8,128)(2,1)S(1)}, u32[]{:S(2)}, u32[]{:S(2)}) collective-permute-start(bf16[32,2048]{1,0:T(8,128)(2,1)} %bitcast.26), channel_id=1, source_target_pairs={{0,16},{8,24},{16,0},{24,8},{1,17},{9,25},{17,1},{25,9},{2,18},{10... | collective-permute-start | bytes 393224 | tf_op jit(solution)/shard_map/ppermute | solution.py:27
  5.7 11.3 %collective-permute-start = (bf16[32,2048]{1,0:T(8,128)(2,1)}, bf16[32,2048]{1,0:T(8,128)(2,1)S(1)}, u32[]{:S(2)}, u32[]{:S(2)}) collective-permute-start(bf16[32,2048]{1,0:T(8,128)(2,1)} %bitcast.27), channel_id=1, source_target_pairs={{0,8},{8,0},{16,24},{24,16},{1,9},{9,1},{17,25},{25,17},{2,10},{10... | collective-permute-start | bytes 393224 | tf_op jit(solution)/shard_map/ppermute | solution.py:27
  28.4 11.2 %collective-permute-start.3 = (bf16[64,3584]{1,0:T(8,128)(2,1)S(1)}, bf16[64,3584]{1,0:T(8,128)(2,1)S(1)}, u32[]{:S(2)}, u32[]{:S(2)}) collective-permute-start(bf16[64,3584]{1,0:T(8,128)(2,1)S(1)} %get-tuple-element.10), channel_id=1, source_target_pairs={{0,2},{2,0},{4,6},{6,4},{1,3},{3,1},{5,7},{7,5},{8,10},{10,8},{12,... | collective-permute-start | bytes 1376264 | tf_op jit(solution)/shard_map/ppermute | solution.py:27
  39.7 8.5 %collective-permute-start.4 = (bf16[32,3584]{1,0:T(8,128)(2,1)S(1)}, bf16[32,3584]{1,0:T(8,128)(2,1)S(1)}, u32[]{:S(2)}, u32[]{:S(2)}) collective-permute-start(bf16[32,3584]{1,0:T(8,128)(2,1)S(1)} %add_convert_fusion.1), channel_id=1, source_target_pairs={{0,4},{2,6},{4,0},{6,2},{1,5},{3,7},{5,1},{7,3},{8,12},{10,14},{12... | collective-permute-start | bytes 688136 | tf_op jit(solution)/shard_map/ppermute | solution.py:27
  41.3 10.9 %collective-permute-start.6 = (bf16[32,3584]{1,0:T(8,128)(2,1)S(1)}, bf16[32,3584]{1,0:T(8,128)(2,1)S(1)}, u32[]{:S(2)}, u32[]{:S(2)}) collective-permute-start(bf16[32,3584]{1,0:T(8,128)(2,1)S(1)} %add_convert_fusion), channel_id=1, source_target_pairs={{0,4},{2,6},{4,0},{6,2},{1,5},{3,7},{5,1},{7,3},{8,12},{10,14},{12... | collective-permute-start | bytes 688136 | tf_op jit(solution)/shard_map/ppermute | solution.py:27
  42.7 12.4 %collective-permute-start.14 = (bf16[32,2048]{1,0:T(8,128)(2,1)S(1)}, bf16[32,2048]{1,0:T(8,128)(2,1)S(1)}, u32[]{:S(2)}, u32[]{:S(2)}) collective-permute-start(bf16[32,2048]{1,0:T(8,128)(2,1)S(1)} %bitcast.30), channel_id=1, source_target_pairs={{0,1},{1,0},{2,3},{3,2},{4,5},{5,4},{6,7},{7,6},{8,9},{9,8},{10,11... | collective-permute-start | bytes 393224 | tf_op jit(solution)/shard_map/ppermute | solution.py:27
  53.6 14.7 %collective-permute-start.19 = (bf16[32,3584]{1,0:T(8,128)(2,1)S(1)}, bf16[32,3584]{1,0:T(8,128)(2,1)S(1)}, u32[]{:S(2)}, u32[]{:S(2)}) collective-permute-start(bf16[32,3584]{1,0:T(8,128)(2,1)S(1)} %get-tuple-element.19.refs_0_), channel_id=1, source_target_pairs={{0,4},{2,6},{4,0},{6,2},{1,5},{3,7},{5,1},{7,3},{8,12},{10,14},{12... | collective-permute-start | bytes 688136 | tf_op jit(solution)/shard_map/ppermute | solution.py:27
  55.2 8.2 %collective-permute-start.17 = (bf16[32,2048]{1,0:T(8,128)(2,1)S(1)}, bf16[32,2048]{1,0:T(8,128)(2,1)S(1)}, u32[]{:S(2)}, u32[]{:S(2)}) collective-permute-start(bf16[32,2048]{1,0:T(8,128)(2,1)S(1)} %collective-permute-done.14.refs_12_), channel_id=1, source_target_pairs={{0,24},{8,16},{16,8},{24,0},{1,25},{9,17},{17,9},{25,1},{2,26},{10... | collective-permute-start | bytes 393224 | tf_op jit(solution)/shard_map/ppermute | solution.py:27
  57.6 10.2 %collective-permute-start.16 = (bf16[32,2048]{1,0:T(8,128)(2,1)S(1)}, bf16[32,2048]{1,0:T(8,128)(2,1)S(1)}, u32[]{:S(2)}, u32[]{:S(2)}) collective-permute-start(bf16[32,2048]{1,0:T(8,128)(2,1)S(1)} %collective-permute-done.14.refs_12_), channel_id=1, source_target_pairs={{0,16},{8,24},{16,0},{24,8},{1,17},{9,25},{17,1},{25,9},{2,18},{10... | collective-permute-start | bytes 393224 | tf_op jit(solution)/shard_map/ppermute | solution.py:27
  57.6 12.5 %collective-permute-start.15 = (bf16[32,2048]{1,0:T(8,128)(2,1)S(1)}, bf16[32,2048]{1,0:T(8,128)(2,1)S(1)}, u32[]{:S(2)}, u32[]{:S(2)}) collective-permute-start(bf16[32,2048]{1,0:T(8,128)(2,1)S(1)} %collective-permute-done.14.refs_12_), channel_id=1, source_target_pairs={{0,8},{8,0},{16,24},{24,16},{1,9},{9,1},{17,25},{25,17},{2,10},{10... | collective-permute-start | bytes 393224 | tf_op jit(solution)/shard_map/ppermute | solution.py:27
  59.5 11.1 %collective-permute-start.21 = (bf16[32,3584]{1,0:T(8,128)(2,1)S(1)}, bf16[32,3584]{1,0:T(8,128)(2,1)S(1)}, u32[]{:S(2)}, u32[]{:S(2)}) collective-permute-start(bf16[32,3584]{1,0:T(8,128)(2,1)S(1)} %get-tuple-element.19.refs_0_), channel_id=1, source_target_pairs={{0,1},{1,0},{2,3},{3,2},{4,5},{5,4},{6,7},{7,6},{8,9},{9,8},{10,11... | collective-permute-start | bytes 688136 | tf_op jit(solution)/shard_map/ppermute | solution.py:27
  63.4 7.3 %collective-permute-start.18 = (bf16[32,3584]{1,0:T(8,128)(2,1)S(1)}, bf16[32,3584]{1,0:T(8,128)(2,1)S(1)}, u32[]{:S(2)}, u32[]{:S(2)}) collective-permute-start(bf16[32,3584]{1,0:T(8,128)(2,1)S(1)} %get-tuple-element.19.refs_0_), channel_id=1, source_target_pairs={{0,2},{2,0},{4,6},{6,4},{1,3},{3,1},{5,7},{7,5},{8,10},{10,8},{12,... | collective-permute-start | bytes 688136 | tf_op jit(solution)/shard_map/ppermute | solution.py:27
  67.8 6.9 %collective-permute-start.8 = (bf16[32,3584]{1,0:T(8,128)(2,1)S(1)}, bf16[32,3584]{1,0:T(8,128)(2,1)S(1)}, u32[]{:S(2)}, u32[]{:S(2)}) collective-permute-start(bf16[32,3584]{1,0:T(8,128)(2,1)S(1)} %get-tuple-element.20.refs_0_), channel_id=1, source_target_pairs={{0,4},{2,6},{4,0},{6,2},{1,5},{3,7},{5,1},{7,3},{8,12},{10,14},{12... | collective-permute-start | bytes 688136 | tf_op jit(solution)/shard_map/ppermute | solution.py:27
  68.3 8.5 %collective-permute-start.23 = (bf16[32,3584]{1,0:T(8,128)(2,1)S(1)}, bf16[32,3584]{1,0:T(8,128)(2,1)S(1)}, u32[]{:S(2)}, u32[]{:S(2)}) collective-permute-start(bf16[32,3584]{1,0:T(8,128)(2,1)S(1)} %collective-permute-done.19.refs_2_), channel_id=1, source_target_pairs={{0,1},{1,0},{2,3},{3,2},{4,5},{5,4},{6,7},{7,6},{8,9},{9,8},{10,11... | collective-permute-start | bytes 688136 | tf_op jit(solution)/shard_map/ppermute | solution.py:27
  70.1 11.6 %collective-permute-start.10 = (bf16[32,3584]{1,0:T(8,128)(2,1)S(1)}, bf16[32,3584]{1,0:T(8,128)(2,1)S(1)}, u32[]{:S(2)}, u32[]{:S(2)}) collective-permute-start(bf16[32,3584]{1,0:T(8,128)(2,1)S(1)} %get-tuple-element.20.refs_0_), channel_id=1, source_target_pairs={{0,1},{1,0},{2,3},{3,2},{4,5},{5,4},{6,7},{7,6},{8,9},{9,8},{10,11... | collective-permute-start | bytes 688136 | tf_op jit(solution)/shard_map/ppermute | solution.py:27
  70.7 11.6 %collective-permute-start.20 = (bf16[32,3584]{1,0:T(8,128)(2,1)S(1)}, bf16[32,3584]{1,0:T(8,128)(2,1)S(1)}, u32[]{:S(2)}, u32[]{:S(2)}) collective-permute-start(bf16[32,3584]{1,0:T(8,128)(2,1)S(1)} %collective-permute-done.19.refs_2_), channel_id=1, source_target_pairs={{0,2},{2,0},{4,6},{6,4},{1,3},{3,1},{5,7},{7,5},{8,10},{10,8},{12,... | collective-permute-start | bytes 688136 | tf_op jit(solution)/shard_map/ppermute | solution.py:27
  70.7 11.1 %collective-permute-start.22 = (bf16[32,3584]{1,0:T(8,128)(2,1)S(1)}, bf16[32,3584]{1,0:T(8,128)(2,1)S(1)}, u32[]{:S(2)}, u32[]{:S(2)}) collective-permute-start(bf16[32,3584]{1,0:T(8,128)(2,1)S(1)} %collective-permute-done.21.refs_4_), channel_id=1, source_target_pairs={{0,2},{2,0},{4,6},{6,4},{1,3},{3,1},{5,7},{7,5},{8,10},{10,8},{12,... | collective-permute-start | bytes 688136 | tf_op jit(solution)/shard_map/ppermute | solution.py:27
  74.7 10.1 %collective-permute-start.12 = (bf16[32,3584]{1,0:T(8,128)(2,1)S(1)}, bf16[32,3584]{1,0:T(8,128)(2,1)S(1)}, u32[]{:S(2)}, u32[]{:S(2)}) collective-permute-start(bf16[32,3584]{1,0:T(8,128)(2,1)S(1)} %collective-permute-done.8.refs_2_), channel_id=1, source_target_pairs={{0,1},{1,0},{2,3},{3,2},{4,5},{5,4},{6,7},{7,6},{8,9},{9,8},{10,11... | collective-permute-start | bytes 688136 | tf_op jit(solution)/shard_map/ppermute | solution.py:27
  76.9 7.9 %collective-permute-start.24 = (bf16[32,3584]{1,0:T(8,128)(2,1)S(1)}, bf16[32,3584]{1,0:T(8,128)(2,1)S(1)}, u32[]{:S(2)}, u32[]{:S(2)}) collective-permute-start(bf16[32,3584]{1,0:T(8,128)(2,1)S(1)} %collective-permute-done.23.refs_6_), channel_id=1, source_target_pairs={{0,2},{2,0},{4,6},{6,4},{1,3},{3,1},{5,7},{7,5},{8,10},{10,8},{12,... | collective-permute-start | bytes 688136 | tf_op jit(solution)/shard_map/ppermute | solution.py:27
  81.8 12.0 %collective-permute-start.7 = (bf16[32,3584]{1,0:T(8,128)(2,1)S(1)}, bf16[32,3584]{1,0:T(8,128)(2,1)S(1)}, u32[]{:S(2)}, u32[]{:S(2)}) collective-permute-start(bf16[32,3584]{1,0:T(8,128)(2,1)S(1)} %get-tuple-element.20.refs_0_), channel_id=1, source_target_pairs={{0,2},{2,0},{4,6},{6,4},{1,3},{3,1},{5,7},{7,5},{8,10},{10,8},{12,... | collective-permute-start | bytes 688136 | tf_op jit(solution)/shard_map/ppermute | solution.py:27
  81.8 12.0 %collective-permute-start.9 = (bf16[32,3584]{1,0:T(8,128)(2,1)S(1)}, bf16[32,3584]{1,0:T(8,128)(2,1)S(1)}, u32[]{:S(2)}, u32[]{:S(2)}) collective-permute-start(bf16[32,3584]{1,0:T(8,128)(2,1)S(1)} %collective-permute-done.8.refs_2_), channel_id=1, source_target_pairs={{0,2},{2,0},{4,6},{6,4},{1,3},{3,1},{5,7},{7,5},{8,10},{10,8},{12,... | collective-permute-start | bytes 688136 | tf_op jit(solution)/shard_map/ppermute | solution.py:27
  82.3 11.5 %collective-permute-start.11 = (bf16[32,3584]{1,0:T(8,128)(2,1)S(1)}, bf16[32,3584]{1,0:T(8,128)(2,1)S(1)}, u32[]{:S(2)}, u32[]{:S(2)}) collective-permute-start(bf16[32,3584]{1,0:T(8,128)(2,1)S(1)} %collective-permute-done.10.refs_4_), channel_id=1, source_target_pairs={{0,2},{2,0},{4,6},{6,4},{1,3},{3,1},{5,7},{7,5},{8,10},{10,8},{12,... | collective-permute-start | bytes 688136 | tf_op jit(solution)/shard_map/ppermute | solution.py:27
  84.7 9.1 %collective-permute-start.13 = (bf16[32,3584]{1,0:T(8,128)(2,1)S(1)}, bf16[32,3584]{1,0:T(8,128)(2,1)S(1)}, u32[]{:S(2)}, u32[]{:S(2)}) collective-permute-start(bf16[32,3584]{1,0:T(8,128)(2,1)S(1)} %collective-permute-done.12.refs_6_), channel_id=1, source_target_pairs={{0,2},{2,0},{4,6},{6,4},{1,3},{3,1},{5,7},{7,5},{8,10},{10,8},{12,... | collective-permute-start | bytes 688136 | tf_op jit(solution)/shard_map/ppermute | solution.py:27
  (7 other events, 191.0 us)

commit v2 on v0

v2 whole, which is shorter than its diff:
```python
import jax
import jax.numpy as jnp
from jax import lax
from jax.experimental import pallas as pl
from jax.experimental.pallas import tpu as pltpu
from jax.sharding import PartitionSpec as P

BLOCK = 128
SUB = 256
IN_TILE = 512
HEAD = 8
TAIL = (4, 4)
OUT_TILE = 256
SMALL_VMEM = 4 * 1024 * 1024
PARTIAL_VMEM = 24 * 1024 * 1024
WEIGHT_VMEM = 48 * 1024 * 1024
bf16 = jnp.bfloat16
f32 = jnp.float32


def swap(x, axis, bit):
    n = lax.axis_size(axis)
    return lax.ppermute(x, axis, [(i, i ^ bit) for i in range(n)])


def dest_slot(v):
    return (v >> 1) | ((v & 1) << 1)


def stack_kernel(pos_ref, g0, g1, g2, g3, out_ref):
    rows = g0.shape[0]
    for s, g in enumerate((g0, g1, g2, g3)):
        at = pl.multiple_of(dest_slot(pos_ref[0] ^ s) * rows, rows)
        out_ref[pl.ds(at, rows), :] = g[...]


def stack(pos, grads):
    rows, d_local = grads[0].shape
    vmem = pl.BlockSpec(memory_space=pltpu.VMEM)
    return pl.pallas_call(
        stack_kernel,
        in_specs=[pl.BlockSpec(memory_space=pltpu.SMEM)] + [vmem] * 4,
        out_specs=vmem,
        out_shape=jax.ShapeDtypeStruct((4 * rows, d_local), bf16),
        compiler_params=pltpu.CompilerParams(vmem_limit_bytes=SMALL_VMEM),
        name="stack_tokens",
    )(pos, *grads)


def fetch_kernel(w_ref, held_ref, done_ref, sems):
    def enter(i):
        at = pl.ds(i * IN_TILE, IN_TILE)
        return pltpu.make_async_copy(w_ref.at[at, :], held_ref.at[at, :], sems.at[i])

    tiles = held_ref.shape[0] // IN_TILE
    for i in range(tiles):
        enter(i).start()
    done_ref[...] = jnp.zeros_like(done_ref)
    for i in range(tiles):
        enter(i).wait()


def fetch(w):
    rows = w.shape[0] // IN_TILE * HEAD // 16 * IN_TILE
    anywhere = pl.BlockSpec(memory_space=pl.ANY)
    return pl.pallas_call(
        fetch_kernel,
        in_specs=[anywhere],
        out_specs=[anywhere, pl.BlockSpec(memory_space=pltpu.VMEM)],
        scratch_shapes=[pltpu.SemaphoreType.DMA((rows // IN_TILE,))],
        out_shape=[pltpu.VMEM((rows, w.shape[1]), bf16), jax.ShapeDtypeStruct((8, BLOCK), f32)],
        compiler_params=pltpu.CompilerParams(vmem_limit_bytes=SMALL_VMEM),
        cost_estimate=pl.CostEstimate(flops=0, bytes_accessed=2 * rows * w.shape[1], transcendentals=0),
        name="fetch_weights",
    )(pltpu.with_memory_space_constraint(w, pltpu.HBM))


def partial_kernel(lhs, mask_ref, head_ref, _, w_ref, stay_ref, next_ref, send_ref, held, sems):
    rows = stay_ref.shape[0]
    first = head_ref.shape[0]
    ends = []
    for t in TAIL:
        ends.append((ends[-1] if ends else first) + w_ref.shape[0] // 16 * t)

    def enter(i):
        start = ends[i - 1] if i else first
        return pltpu.make_async_copy(
            w_ref.at[pl.ds(start, ends[i] - start), :],
            held.at[pl.ds(start - first, ends[i] - start), :],
            sems.at[i],
        )

    for i in range(len(ends)):
        enter(i).start()
    for k in range(w_ref.shape[0] // SUB):
        parts = []
        for j in range(SUB // BLOCK):
            r = k * (SUB // BLOCK) + j
            if r * BLOCK < first:
                w = head_ref[r * BLOCK : (r + 1) * BLOCK, :]
            else:
                if r * BLOCK in [first] + ends[:-1]:
                    enter(([first] + ends).index(r * BLOCK)).wait()
                w = held[r * BLOCK - first : (r + 1) * BLOCK - first, :]
            parts.append(w * mask_ref[r : r + 1, :].astype(bf16))
        out = lax.dot_general(
            jnp.concatenate(parts, axis=0),
            lhs[...],
            (((1,), (1,)), ((), ())),
            preferred_element_type=f32,
        ).T.astype(bf16)
        at = slice(k * SUB, (k + 1) * SUB)
        stay_ref[:, at] = out[:rows]
        next_ref[:, at] = out[rows : 2 * rows]
        send_ref[:, at] = out[2 * rows :]


def partial_sums(tokens, mask_rows, head, mark, w):
    f_local, d_local = w.shape
    rows = tokens.shape[0] // 4
    vmem = pl.BlockSpec(memory_space=pltpu.VMEM)
    return pl.pallas_call(
        partial_kernel,
        in_specs=[vmem] * 3 + [pl.BlockSpec(memory_space=pl.ANY)] * 2,
        out_specs=[vmem] * 3,
        scratch_shapes=[
            pltpu.VMEM((f_local - head.shape[0], d_local), bf16),
            pltpu.SemaphoreType.DMA((len(TAIL),)),
        ],
        out_shape=[
            jax.ShapeDtypeStruct((rows, f_local), bf16),
            jax.ShapeDtypeStruct((rows, f_local), bf16),
            jax.ShapeDtypeStruct((2 * rows, f_local), bf16),
        ],
        compiler_params=pltpu.CompilerParams(vmem_limit_bytes=PARTIAL_VMEM),
        cost_estimate=pl.CostEstimate(
            flops=2 * 4 * rows * f_local * d_local, bytes_accessed=2 * f_local * d_local, transcendentals=0
        ),
        name="partial_sums",
    )(
        tokens,
        mask_rows,
        pltpu.with_memory_space_constraint(head, pltpu.VMEM),
        mark,
        pltpu.with_memory_space_constraint(w, pltpu.HBM),
    )


def weight_kernel(*refs):
    acts, tokens = refs[:8], refs[8:10]
    mask_ref, out_ref, held, sems = refs[10:]
    f_local = acts[0].shape[1]
    tiles = f_local // OUT_TILE

    def leave(i):
        return pltpu.make_async_copy(
            held.at[i], out_ref.at[pl.ds(i * OUT_TILE, OUT_TILE), :], sems.at[i]
        )

    rhs = jnp.concatenate([t[...] for t in tokens], axis=0)
    for i in range(tiles):
        at = slice(i * OUT_TILE, (i + 1) * OUT_TILE)
        lhs = jnp.concatenate([a[:, at] for a in acts], axis=0)
        total = lax.dot_general(lhs, rhs, (((0,), (0,)), ((), ())), preferred_element_type=f32)
        for k in range(OUT_TILE // BLOCK):
            r = i * (OUT_TILE // BLOCK) + k
            part = slice(k * BLOCK, (k + 1) * BLOCK)
            held[i, part, :] = (total[part, :] * mask_ref[r : r + 1, :]).astype(bf16)
        leave(i).start()
    for i in range(tiles):
        leave(i).wait()


def weight_grad(acts, tokens, mask_scaled):
    f_local = acts[0].shape[1]
    every, d_local = 2 * tokens[0].shape[0], tokens[0].shape[1]
    vmem = pl.BlockSpec(memory_space=pltpu.VMEM)
    tiles = f_local // OUT_TILE
    return pl.pallas_call(
        weight_kernel,
        in_specs=[vmem] * 11,
        out_specs=pl.BlockSpec(memory_space=pl.ANY),
        scratch_shapes=[
            pltpu.VMEM((tiles, OUT_TILE, d_local), bf16),
            pltpu.SemaphoreType.DMA((tiles,)),
        ],
        out_shape=jax.ShapeDtypeStruct((f_local, d_local), bf16),
        compiler_params=pltpu.CompilerParams(vmem_limit_bytes=WEIGHT_VMEM),
        cost_estimate=pl.CostEstimate(
            flops=2 * every * f_local * d_local, bytes_accessed=2 * f_local * d_local, transcendentals=0
        ),
        name="weight_grad",
    )(*acts, *tokens, mask_scaled)


def activation(gate, up):
    gate, up = gate.astype(f32), up.astype(f32)
    return (gate * jax.nn.sigmoid(gate) * up).astype(bf16)


def local(grad_out, gate_pre, up_pre, w_down, block_mask):
    f_local, d_local = w_down.shape
    row, col = lax.axis_index("row"), lax.axis_index("col")
    scale = 1.0 / jnp.sqrt(f32(lax.axis_size("dp") * lax.axis_size("row") * grad_out.shape[1]))
    own_mask = lax.dynamic_slice(
        block_mask,
        (row * (f_local // BLOCK), col * (d_local // BLOCK)),
        (f_local // BLOCK, d_local // BLOCK),
    )
    keep = jnp.repeat((own_mask > 0).astype(f32), BLOCK, axis=1)
    keep_scaled = keep * scale

    gate, up = gate_pre[0], up_pre[0]
    own = grad_out[0]
    rows = own.shape[0]

    grads = [own] + [swap(own, "row", s) for s in (1, 2, 3)]
    act = activation(gate, up)
    act_x, act_y = swap(act, "dp", 1), swap(act, "col", 2)

    pos = jnp.full((1,), row ^ col, jnp.int32)
    tokens = stack(pos, grads)
    head, mark = fetch(w_down)
    act_c = swap(act, "col", 1)
    tokens, act, act_c, act_x, act_y, keep, keep_scaled, mark = lax.optimization_barrier(
        (tokens, act, act_c, act_x, act_y, keep, keep_scaled, mark)
    )

    tokens_x, act_xy = swap(tokens, "dp", 1), swap(act_x, "col", 2)
    stay, onward, send = partial_sums(tokens, keep, head, mark, w_down)
    send, tokens_x, act_xy = lax.optimization_barrier((send, tokens_x, act_xy))

    got = swap(send, "col", 1)
    act_yc, act_xc, act_xyc = [swap(a, "col", 1) for a in (act_y, act_x, act_xy)]
    mine = stay.astype(f32) + got[:rows].astype(f32)
    theirs = (onward.astype(f32) + got[rows:].astype(f32)).astype(bf16)
    last = swap(theirs, "col", 2)

    acts = [act, act_y, act_c, act_yc, act_x, act_xy, act_xc, act_xyc]
    grad_down = weight_grad(acts, [tokens, tokens_x], keep_scaled)

    dact = mine + last.astype(f32)
    gate, up = gate.astype(f32), up.astype(f32)
    sig = jax.nn.sigmoid(gate)
    grad_gate = (dact * up * sig * (1.0 + gate * (1.0 - sig))).astype(bf16)
    grad_up = (dact * gate * sig).astype(bf16)
    return grad_gate[None], grad_up[None], grad_down


def general(grad_out, gate_pre, up_pre, w_down, block_mask):
    f_local, d_local = w_down.shape
    row_block = (lax.axis_index("row") * f_local + jnp.arange(f_local)) // BLOCK
    col_block = (lax.axis_index("col") * d_local + jnp.arange(d_local)) // BLOCK
    keep = block_mask[row_block][:, col_block] > 0
    w_kept = jnp.where(keep, w_down, jnp.zeros_like(w_down))
    gate, up = gate_pre[0].astype(f32), up_pre[0].astype(f32)
    sig = jax.nn.sigmoid(gate)
    act = (gate * sig * up).astype(bf16)
    grads = lax.all_gather(grad_out[0], "row", axis=0, tiled=True)
    partial = lax.dot_general(
        grads, w_kept, (((1,), (1,)), ((), ())), preferred_element_type=f32
    ).astype(bf16)
    dact = lax.psum_scatter(partial, "col", scatter_dimension=0, tiled=True).astype(f32)
    acts = lax.all_gather(act, ("dp", "col"), axis=0, tiled=True)
    every = lax.all_gather(grads, "dp", axis=0, tiled=True)
    total = lax.dot_general(acts, every, (((0,), (0,)), ((), ())), preferred_element_type=f32)
    scale = 1.0 / jnp.sqrt(f32(every.shape[0]))
    grad_down = jnp.where(keep, total * scale, jnp.zeros_like(total)).astype(bf16)
    grad_gate = (dact * up * sig * (1.0 + gate * (1.0 - sig))).astype(bf16)
    grad_up = (dact * gate * sig).astype(bf16)
    return grad_gate[None], grad_up[None], grad_down


def solution(mesh):
    placed = (
        P("dp", "row", "col"),
        P("dp", "col", "row"),
        P("dp", "col", "row"),
        P("row", "col"),
        P(),
    )
    size = dict(mesh.shape)
    pairwise = size["row"] == 4 and size["col"] == 4 and size["dp"] == 2

    def run(grad_out, gate_pre, up_pre, w_down, block_mask):
        f_local, d_local = w_down.shape
        rows = grad_out.shape[1]
        fits = pairwise and rows == gate_pre.shape[1] and rows % 16 == 0
        fits = fits and f_local % 1024 == 0 and d_local % BLOCK == 0
        step = local if fits else general
        return step(grad_out, gate_pre, up_pre, w_down, block_mask)

    return jax.shard_map(
        run,
        mesh=mesh,
        in_specs=placed,
        out_specs=(P("dp", "col", "row"), P("dp", "col", "row"), P("row", "col")),
        check_vma=False,
    )
```

time: 831 us -> 50.2 us (0.06)
  waiting for transfers between devices: 701 us -> 6.79 us
  matrix products: 68 us -> 0 us
  Pallas kernels: 0 us -> 24.5 us
  other arithmetic: 27.4 us -> 4 us
  blocking collectives: 17.6 us -> 0 us
  between operations: 13.8 us -> 0.75 us
  starting transfers between devices: 0.12 us -> 12.8 us
    psum x1 -> x0, waiting for transfers between devices: 648 us -> none  [local(): lax.psum(weight_grad.astype(jnp.bfloat16), 'dp').astype(jnp.float32)]
    dot_general x4 -> x0, matrix products: 68 us -> none  [the longest x1 30.8 us: local_keep(): return jnp.dot(picked, col_pick, precision=lax.Precision.HIGHEST)]
    reduce_scatter x1 -> x0, waiting for transfers between devices: 31.7 us -> none  [local(): lax.psum_scatter(partial_value.astype(jnp.bfloat16), 'col', scatter_dimen...]
    convert_element_type x2 -> x3, other arithmetic: 27.4 us -> 2.32 us  [the longest x1 1.42 us: activation(): return (gate * jax.nn.sigmoid(gate) * up).astype(bf16)]
    pallas_call x0 -> x4, Pallas kernels: none -> 24.5 us  [the longest x1 10.3 us: weight_grad(): pl.pallas_call(weight_kernel, in_specs=[vmem] * 11, out_specs=pl.BlockSpe...]
    all_gather x1 -> x0, waiting for transfers between devices: 21.2 us -> none  [local(): act_all = lax.all_gather(act, 'col', axis=0, tiled=True)]
    all_gather x1 -> x0, blocking collectives: 17.6 us -> none  [local(): grad_all = lax.all_gather(grad_out, 'row', axis=1, tiled=True)]
    ppermute x0 -> x13, starting transfers between devices: none -> 12.8 us  [swap(): return lax.ppermute(x, axis, [(i, i ^ bit) for i in range(n)])]
  transfers between devices with their start and end apart: 3 -> 13, of which waited for: 3 -> 8; matrix products, arithmetic and copies ran while one was open for 0% -> 6% of each run, Pallas kernels for 0% -> 50%
where the time goes in v2:
time: 50.2 us; the launch traced here: 49.3 us
  Pallas kernels  24.5 us (49%)
  starting transfers between devices  12.8 us (25%)
  waiting for transfers between devices  6.79 us (14%)
  other arithmetic  4 us (8%)
  between operations  0.75 us (1%)
    ppermute x13, starting transfers between devices, swap(): return lax.ppermute(x, axis, [(i, i ^ bit) for i in range(n)])  12.8 us
    pallas_call x1, Pallas kernels, weight_grad(): pl.pallas_call(weight_kernel, in_specs=[vmem] * 11, out_specs=pl.BlockSpe...  10.3 us
    pallas_call x1, Pallas kernels, partial_sums(): pl.pallas_call(partial_kernel, in_specs=[vmem] * 3 + [pl.BlockSpec(memory...  8.85 us
    ppermute x13, waiting for transfers between devices, swap(): return lax.ppermute(x, axis, [(i, i ^ bit) for i in range(n)])  6.79 us
    pallas_call x1, Pallas kernels, fetch(): pl.pallas_call(fetch_kernel, in_specs=[anywhere], out_specs=[anywhere, pl...  5.32 us
    broadcast_in_dim x1, other arithmetic, local(): return (grad_gate[None], grad_up[None], grad_down)  1.51 us
    convert_element_type x1, other arithmetic, activation(): return (gate * jax.nn.sigmoid(gate) * up).astype(bf16)  1.42 us
  transfers between devices with their start and end apart: 13, of which 8 were waited for; matrix products, arithmetic and copies ran while one was open for 6% of the time, Pallas kernels for 50%

profile of v2, /device:TPU:0, one launch (start us, length us, event | category | flops | bytes accessed | tf_op | source)
XLA Modules:
  0.0 49.3 jit_solution(15259084665031579985)
XLA Ops:
  0.6 5.1 %collective-permute-start.2 = (bf16[32,2048]{1,0:T(8,128)(2,1)}, bf16[32,2048]{1,0:T(8,128)(2,1)S(1)}, u32[]{:S(2)}, u32[]{:S(2)}) collective-permute-start(bf16[32,2048]{1,0:T(8,128)(2,1)} %bitcast.28), channel_id=1, source_target_pairs={{0,24},{8,16},{16,8},{24,0},{1,25},{9,17},{17,9},{25,1},{2,26},{10... | collective-permute-start | bytes 393224 | tf_op jit(solution)/shard_map/ppermute | solution.py:23
  5.8 0.6 %collective-permute-start = (bf16[32,2048]{1,0:T(8,128)(2,1)}, bf16[32,2048]{1,0:T(8,128)(2,1)S(1)}, u32[]{:S(2)}, u32[]{:S(2)}) collective-permute-start(bf16[32,2048]{1,0:T(8,128)(2,1)} %bitcast.30), channel_id=1, source_target_pairs={{0,8},{8,0},{16,24},{24,16},{1,9},{9,1},{17,25},{25,17},{2,10},{10... | collective-permute-start | bytes 393224 | tf_op jit(solution)/shard_map/ppermute | solution.py:23
  6.4 1.4 %fusion.refs_0_ = bf16[32,7168]{1,0:T(8,128)(2,1)S(1)} fusion(bf16[1,32,7168]{2,1,0:T(8,128)(2,1)} %param.7, bf16[1,32,7168]{2,1,0:T(8,128)(2,1)} %param.6), kind=kLoop, calls=%fused_computation.6 | loop fusion | flops 1835008 | bytes 1376256 | tf_op jit(solution)/shard_map/convert_element_type | solution.py:198
  7.8 1.7 %collective-permute-start.5 = (bf16[32,7168]{1,0:T(8,128)(2,1)S(1)}, bf16[32,7168]{1,0:T(8,128)(2,1)S(1)}, u32[]{:S(2)}, u32[]{:S(2)}) collective-permute-start(bf16[32,7168]{1,0:T(8,128)(2,1)S(1)} %fusion.refs_0_), channel_id=1, source_target_pairs={{0,4},{2,6},{4,0},{6,2},{1,5},{3,7},{5,1},{7,3},{8,12},{10,14},{12... | collective-permute-start | bytes 1376264 | tf_op jit(solution)/shard_map/ppermute | solution.py:23
  9.6 1.5 %collective-permute-start.4 = (bf16[32,7168]{1,0:T(8,128)(2,1)S(1)}, bf16[32,7168]{1,0:T(8,128)(2,1)S(1)}, u32[]{:S(2)}, u32[]{:S(2)}) collective-permute-start(bf16[32,7168]{1,0:T(8,128)(2,1)S(1)} %fusion.refs_0_), channel_id=1, source_target_pairs={{0,1},{1,0},{2,3},{3,2},{4,5},{5,4},{6,7},{7,6},{8,9},{9,8},{10,11... | collective-permute-start | bytes 1376264 | tf_op jit(solution)/shard_map/ppermute | solution.py:23
  11.0 0.8 %fusion.12 = f32[56,16]{0,1:T(8,128)S(1)} fusion(s32[224,64]{0,1:T(8,128)} %param.9, s32[]{:T(128)S(6)} %select_n.6, s32[]{:T(128)S(6)} %select_n.7), kind=kLoop, calls=%fused_computation.23 | loop fusion | flops 1792 | bytes 7176 | tf_op jit(solution)/shard_map/convert_element_type | solution.py:210
  12.0 0.2 broadcast_in_dim.13
  12.5 5.3 %fetch_weights.1 = (bf16[3584,2048]{1,0:T(8,128)(2,1)S(1)}, f32[8,128]{1,0:T(8,128)S(1)}) custom-call(bf16[7168,2048]{1,0:T(8,128)(2,1)} %w_ref.3), custom_call_target="tpu_custom_call" | custom-call | bytes 14680064 | tf_op jit(solution)/shard_map/fetch_weights/pallas_call | solution.py:66
  17.9 1.7 %collective-permute-done.5.refs_1_ = bf16[32,7168]{1,0:T(8,128)(2,1)S(1)} collective-permute-done((bf16[32,7168]{1,0:T(8,128)(2,1)S(1)}, bf16[32,7168]{1,0:T(8,128)(2,1)S(1)}, u32[]{:S(2)}, u32[]{:S(2)}) %collective-permute-start.5) | collective-permute-done | bytes 458784 | tf_op jit(solution)/shard_map/ppermute | solution.py:23
  19.6 1.2 %collective-permute-done.4.refs_4_ = bf16[32,7168]{1,0:T(8,128)(2,1)S(1)} collective-permute-done((bf16[32,7168]{1,0:T(8,128)(2,1)S(1)}, bf16[32,7168]{1,0:T(8,128)(2,1)S(1)}, u32[]{:S(2)}, u32[]{:S(2)}) %collective-permute-start.4) | collective-permute-done | bytes 458784 | tf_op jit(solution)/shard_map/ppermute | solution.py:23
  20.8 1.5 %collective-permute-start.6 = (bf16[128,2048]{1,0:T(8,128)(2,1)S(1)}, bf16[128,2048]{1,0:T(8,128)(2,1)S(1)}, u32[]{:S(2)}, u32[]{:S(2)}) collective-permute-start(bf16[128,2048]{1,0:T(8,128)(2,1)S(1)} %stack_tokens.1.lhs.refs_8_), channel_id=1, source_target_pairs={{0,1},{1,0},{2,3},{3,2},{4,5},{5,4},{6,7},{7,6},{8,9},{9,8},{10,11... | collective-permute-start | bytes 1572872 | tf_op jit(solution)/shard_map/ppermute | solution.py:23
  22.3 0.5 %collective-permute-start.7 = (bf16[32,7168]{1,0:T(8,128)(2,1)S(1)}, bf16[32,7168]{1,0:T(8,128)(2,1)S(1)}, u32[]{:S(2)}, u32[]{:S(2)}) collective-permute-start(bf16[32,7168]{1,0:T(8,128)(2,1)S(1)} %collective-permute-done.4.refs_4_), channel_id=1, source_target_pairs={{0,4},{2,6},{4,0},{6,2},{1,5},{3,7},{5,1},{7,3},{8,12},{10,14},{12... | collective-permute-start | bytes 1376264 | tf_op jit(solution)/shard_map/ppermute | solution.py:23
  22.8 8.8 %partial_sums.1 = (bf16[32,7168]{1,0:T(8,128)(2,1)S(1)}, bf16[32,7168]{1,0:T(8,128)(2,1)S(1)}, bf16[64,7168]{1,0:T(8,128)(2,1)S(1)}) custom-call(bf16[128,2048]{1,0:T(8,128)(2,1)S(1)} %stack_tokens.1.lhs.refs_8_, f32[56,2048]{1,0:T(8,128)S(1)} %bitcast.27, bf16[3584,2048]{1,0:T(8,128)(2,1)S(1)} %get-tuple-element.22.head_ref, ...), custom_call_target="tpu_custom_call" | custom-call | flops 3758096384 | bytes 29360128 | tf_op jit(solution)/shard_map/partial_sums/pallas_call | solution.py:122
  31.7 0.7 %collective-permute-done.7.refs_5_ = bf16[32,7168]{1,0:T(8,128)(2,1)S(1)} collective-permute-done((bf16[32,7168]{1,0:T(8,128)(2,1)S(1)}, bf16[32,7168]{1,0:T(8,128)(2,1)S(1)}, u32[]{:S(2)}, u32[]{:S(2)}) %collective-permute-start.7) | collective-permute-done | bytes 458784 | tf_op jit(solution)/shard_map/ppermute | solution.py:23
  32.4 0.2 collective-permute-done.6.refs_9_
  32.6 0.5 %collective-permute-start.11 = (bf16[32,7168]{1,0:T(8,128)(2,1)S(1)}, bf16[32,7168]{1,0:T(8,128)(2,1)S(1)}, u32[]{:S(2)}, u32[]{:S(2)}) collective-permute-start(bf16[32,7168]{1,0:T(8,128)(2,1)S(1)} %collective-permute-done.4.refs_4_), channel_id=1, source_target_pairs={{0,2},{2,0},{4,6},{6,4},{1,3},{3,1},{5,7},{7,5},{8,10},{10,8},{12,... | collective-permute-start | bytes 1376264 | tf_op jit(solution)/shard_map/ppermute | solution.py:23
  33.1 0.5 %collective-permute-start.12 = (bf16[32,7168]{1,0:T(8,128)(2,1)S(1)}, bf16[32,7168]{1,0:T(8,128)(2,1)S(1)}, u32[]{:S(2)}, u32[]{:S(2)}) collective-permute-start(bf16[32,7168]{1,0:T(8,128)(2,1)S(1)} %collective-permute-done.7.refs_5_), channel_id=1, source_target_pairs={{0,2},{2,0},{4,6},{6,4},{1,3},{3,1},{5,7},{7,5},{8,10},{10,8},{12,... | collective-permute-start | bytes 1376264 | tf_op jit(solution)/shard_map/ppermute | solution.py:23
  33.6 1.5 %collective-permute-done.8 = bf16[64,7168]{1,0:T(8,128)(2,1)S(1)} collective-permute-done((bf16[64,7168]{1,0:T(8,128)(2,1)S(1)}, bf16[64,7168]{1,0:T(8,128)(2,1)S(1)}, u32[]{:S(2)}, u32[]{:S(2)}) %collective-permute-start.8) | collective-permute-done | bytes 917536 | tf_op jit(solution)/shard_map/ppermute | solution.py:23
  35.2 0.8 %collective-permute-start.9 = (bf16[32,7168]{1,0:T(8,128)(2,1)S(1)}, bf16[32,7168]{1,0:T(8,128)(2,1)S(1)}, u32[]{:S(2)}, u32[]{:S(2)}) collective-permute-start(bf16[32,7168]{1,0:T(8,128)(2,1)S(1)} %add_convert_fusion), channel_id=1, source_target_pairs={{0,4},{2,6},{4,0},{6,2},{1,5},{3,7},{5,1},{7,3},{8,12},{10,14},{12... | collective-permute-start | bytes 1376264 | tf_op jit(solution)/shard_map/ppermute | solution.py:23
  35.9 0.4 collective-permute-done.10.refs_3_
  36.4 0.7 %collective-permute-done.12.refs_7_ = bf16[32,7168]{1,0:T(8,128)(2,1)S(1)} collective-permute-done((bf16[32,7168]{1,0:T(8,128)(2,1)S(1)}, bf16[32,7168]{1,0:T(8,128)(2,1)S(1)}, u32[]{:S(2)}, u32[]{:S(2)}) %collective-permute-start.12) | collective-permute-done | bytes 458784 | tf_op jit(solution)/shard_map/ppermute | solution.py:23
  37.0 10.3 %weight_grad.1 = bf16[7168,2048]{1,0:T(8,128)(2,1)} custom-call(bf16[32,7168]{1,0:T(8,128)(2,1)S(1)} %fusion.refs_0_, bf16[32,7168]{1,0:T(8,128)(2,1)S(1)} %collective-permute-done.5.refs_1_, bf16[32,7168]{1,0:T(8,128)(2,1)S(1)} %collective-permute-done.3.refs_2_, bf16[32,7168]{1,0:T(8,128)(2,1)S(1)} %collective-permute-done.10.refs_3_, ...), custom_call_target="tpu_custom_call" | custom-call | flops 7516192768 | bytes 29360128 | tf_op jit(solution)/shard_map/weight_grad/pallas_call | solution.py:179
  47.4 0.4 collective-permute-done.9
  47.8 1.5 %fusion.10 = (bf16[1,32,7168]{2,1,0:T(8,128)(2,1)}, bf16[1,32,7168]{2,1,0:T(8,128)(2,1)}) fusion(bf16[1,32,7168]{2,1,0:T(8,128)(2,1)S(1)} %copy-done.1, bf16[32,7168]{1,0:T(8,128)(2,1)S(1)} %collective-permute-done.9, bf16[32,7168]{1,0:T(8,128)(2,1)S(1)} %get-tuple-element.24, bf16[64,7168]{1,0:T(8,128)(2,1)S(1)} %collective-permute-done.8, ...), kind=kLoop, calls=%fused_computation.19 | loop fusion | flops 4587520 | bytes 3211264 | tf_op jit(solution)/shard_map/broadcast_in_dim | solution.py:247
  (20 shorter events, 0.6 us)
Async XLA Ops:
  0.6 17.2 %copy-start = (bf16[1,32,2048]{2,1,0:T(8,128)(2,1)S(1)}, bf16[1,32,2048]{2,1,0:T(8,128)(2,1)}, u32[]{:S(2)}) copy-start(bf16[1,32,2048]{2,1,0:T(8,128)(2,1)} %param.5) | copy-start | bytes 393220
  0.6 11.3 %collective-permute-start.2 = (bf16[32,2048]{1,0:T(8,128)(2,1)}, bf16[32,2048]{1,0:T(8,128)(2,1)S(1)}, u32[]{:S(2)}, u32[]{:S(2)}) collective-permute-start(bf16[32,2048]{1,0:T(8,128)(2,1)} %bitcast.28), channel_id=1, source_target_pairs={{0,24},{8,16},{16,8},{24,0},{1,25},{9,17},{17,9},{25,1},{2,26},{10... | collective-permute-start | bytes 393224 | tf_op jit(solution)/shard_map/ppermute | solution.py:23
  5.8 12.1 %collective-permute-start.1 = (bf16[32,2048]{1,0:T(8,128)(2,1)}, bf16[32,2048]{1,0:T(8,128)(2,1)S(1)}, u32[]{:S(2)}, u32[]{:S(2)}) collective-permute-start(bf16[32,2048]{1,0:T(8,128)(2,1)} %bitcast.29), channel_id=1, source_target_pairs={{0,16},{8,24},{16,0},{24,8},{1,17},{9,25},{17,1},{25,9},{2,18},{10... | collective-permute-start | bytes 393224 | tf_op jit(solution)/shard_map/ppermute | solution.py:23
  5.8 12.1 %collective-permute-start = (bf16[32,2048]{1,0:T(8,128)(2,1)}, bf16[32,2048]{1,0:T(8,128)(2,1)S(1)}, u32[]{:S(2)}, u32[]{:S(2)}) collective-permute-start(bf16[32,2048]{1,0:T(8,128)(2,1)} %bitcast.30), channel_id=1, source_target_pairs={{0,8},{8,0},{16,24},{24,16},{1,9},{9,1},{17,25},{25,17},{2,10},{10... | collective-permute-start | bytes 393224 | tf_op jit(solution)/shard_map/ppermute | solution.py:23
  7.8 11.8 %collective-permute-start.5 = (bf16[32,7168]{1,0:T(8,128)(2,1)S(1)}, bf16[32,7168]{1,0:T(8,128)(2,1)S(1)}, u32[]{:S(2)}, u32[]{:S(2)}) collective-permute-start(bf16[32,7168]{1,0:T(8,128)(2,1)S(1)} %fusion.refs_0_), channel_id=1, source_target_pairs={{0,4},{2,6},{4,0},{6,2},{1,5},{3,7},{5,1},{7,3},{8,12},{10,14},{12... | collective-permute-start | bytes 1376264 | tf_op jit(solution)/shard_map/ppermute | solution.py:23
  9.6 11.3 %collective-permute-start.4 = (bf16[32,7168]{1,0:T(8,128)(2,1)S(1)}, bf16[32,7168]{1,0:T(8,128)(2,1)S(1)}, u32[]{:S(2)}, u32[]{:S(2)}) collective-permute-start(bf16[32,7168]{1,0:T(8,128)(2,1)S(1)} %fusion.refs_0_), channel_id=1, source_target_pairs={{0,1},{1,0},{2,3},{3,2},{4,5},{5,4},{6,7},{7,6},{8,9},{9,8},{10,11... | collective-permute-start | bytes 1376264 | tf_op jit(solution)/shard_map/ppermute | solution.py:23
  11.9 8.9 %collective-permute-start.3 = (bf16[32,7168]{1,0:T(8,128)(2,1)S(1)}, bf16[32,7168]{1,0:T(8,128)(2,1)S(1)}, u32[]{:S(2)}, u32[]{:S(2)}) collective-permute-start(bf16[32,7168]{1,0:T(8,128)(2,1)S(1)} %fusion.refs_0_), channel_id=1, source_target_pairs={{0,2},{2,0},{4,6},{6,4},{1,3},{3,1},{5,7},{7,5},{8,10},{10,8},{12,... | collective-permute-start | bytes 1376264 | tf_op jit(solution)/shard_map/ppermute | solution.py:23
  20.8 11.8 %collective-permute-start.6 = (bf16[128,2048]{1,0:T(8,128)(2,1)S(1)}, bf16[128,2048]{1,0:T(8,128)(2,1)S(1)}, u32[]{:S(2)}, u32[]{:S(2)}) collective-permute-start(bf16[128,2048]{1,0:T(8,128)(2,1)S(1)} %stack_tokens.1.lhs.refs_8_), channel_id=1, source_target_pairs={{0,1},{1,0},{2,3},{3,2},{4,5},{5,4},{6,7},{7,6},{8,9},{9,8},{10,11... | collective-permute-start | bytes 1572872 | tf_op jit(solution)/shard_map/ppermute | solution.py:23
  22.3 10.1 %collective-permute-start.7 = (bf16[32,7168]{1,0:T(8,128)(2,1)S(1)}, bf16[32,7168]{1,0:T(8,128)(2,1)S(1)}, u32[]{:S(2)}, u32[]{:S(2)}) collective-permute-start(bf16[32,7168]{1,0:T(8,128)(2,1)S(1)} %collective-permute-done.4.refs_4_), channel_id=1, source_target_pairs={{0,4},{2,6},{4,0},{6,2},{1,5},{3,7},{5,1},{7,3},{8,12},{10,14},{12... | collective-permute-start | bytes 1376264 | tf_op jit(solution)/shard_map/ppermute | solution.py:23
  22.8 25.0 %copy-start.1 = (bf16[1,32,7168]{2,1,0:T(8,128)(2,1)S(1)}, bf16[1,32,7168]{2,1,0:T(8,128)(2,1)}, u32[]{:S(2)}) copy-start(bf16[1,32,7168]{2,1,0:T(8,128)(2,1)} %param.6) | copy-start | bytes 1376260
  22.8 25.0 %copy-start.2 = (bf16[1,32,7168]{2,1,0:T(8,128)(2,1)S(1)}, bf16[1,32,7168]{2,1,0:T(8,128)(2,1)}, u32[]{:S(2)}) copy-start(bf16[1,32,7168]{2,1,0:T(8,128)(2,1)} %param.7) | copy-start | bytes 1376260
  32.6 2.5 %collective-permute-start.8 = (bf16[64,7168]{1,0:T(8,128)(2,1)S(1)}, bf16[64,7168]{1,0:T(8,128)(2,1)S(1)}, u32[]{:S(2)}, u32[]{:S(2)}) collective-permute-start(bf16[64,7168]{1,0:T(8,128)(2,1)S(1)} %get-tuple-element.27), channel_id=1, source_target_pairs={{0,2},{2,0},{4,6},{6,4},{1,3},{3,1},{5,7},{7,5},{8,10},{10,8},{12,... | collective-permute-start | bytes 2752520 | tf_op jit(solution)/shard_map/ppermute | solution.py:23
  32.6 3.8 %collective-permute-start.11 = (bf16[32,7168]{1,0:T(8,128)(2,1)S(1)}, bf16[32,7168]{1,0:T(8,128)(2,1)S(1)}, u32[]{:S(2)}, u32[]{:S(2)}) collective-permute-start(bf16[32,7168]{1,0:T(8,128)(2,1)S(1)} %collective-permute-done.4.refs_4_), channel_id=1, source_target_pairs={{0,2},{2,0},{4,6},{6,4},{1,3},{3,1},{5,7},{7,5},{8,10},{10,8},{12,... | collective-permute-start | bytes 1376264 | tf_op jit(solution)/shard_map/ppermute | solution.py:23
  33.1 3.3 %collective-permute-start.10 = (bf16[32,7168]{1,0:T(8,128)(2,1)S(1)}, bf16[32,7168]{1,0:T(8,128)(2,1)S(1)}, u32[]{:S(2)}, u32[]{:S(2)}) collective-permute-start(bf16[32,7168]{1,0:T(8,128)(2,1)S(1)} %collective-permute-done.5.refs_1_), channel_id=1, source_target_pairs={{0,2},{2,0},{4,6},{6,4},{1,3},{3,1},{5,7},{7,5},{8,10},{10,8},{12,... | collective-permute-start | bytes 1376264 | tf_op jit(solution)/shard_map/ppermute | solution.py:23
  33.1 3.9 %collective-permute-start.12 = (bf16[32,7168]{1,0:T(8,128)(2,1)S(1)}, bf16[32,7168]{1,0:T(8,128)(2,1)S(1)}, u32[]{:S(2)}, u32[]{:S(2)}) collective-permute-start(bf16[32,7168]{1,0:T(8,128)(2,1)S(1)} %collective-permute-done.7.refs_5_), channel_id=1, source_target_pairs={{0,2},{2,0},{4,6},{6,4},{1,3},{3,1},{5,7},{7,5},{8,10},{10,8},{12,... | collective-permute-start | bytes 1376264 | tf_op jit(solution)/shard_map/ppermute | solution.py:23
  35.2 12.6 %collective-permute-start.9 = (bf16[32,7168]{1,0:T(8,128)(2,1)S(1)}, bf16[32,7168]{1,0:T(8,128)(2,1)S(1)}, u32[]{:S(2)}, u32[]{:S(2)}) collective-permute-start(bf16[32,7168]{1,0:T(8,128)(2,1)S(1)} %add_convert_fusion), channel_id=1, source_target_pairs={{0,4},{2,6},{4,0},{6,2},{1,5},{3,7},{5,1},{7,3},{8,12},{10,14},{12... | collective-permute-start | bytes 1376264 | tf_op jit(solution)/shard_map/ppermute | solution.py:23

commit v3 on v2

--- a/solution.py
+++ b/solution.py
@@ -9,7 +9,6 @@
 SUB = 256
 IN_TILE = 512
 HEAD = 8
-TAIL = (4, 4)
 OUT_TILE = 256
 SMALL_VMEM = 4 * 1024 * 1024
 PARTIAL_VMEM = 24 * 1024 * 1024
@@ -61,7 +60,7 @@
 
 
 def fetch(w):
-    rows = w.shape[0] // IN_TILE * HEAD // 16 * IN_TILE
+    rows = w.shape[0] // IN_TILE * HEAD // 14 * IN_TILE
     anywhere = pl.BlockSpec(memory_space=pl.ANY)
     return pl.pallas_call(
         fetch_kernel,
@@ -78,9 +77,7 @@
 def partial_kernel(lhs, mask_ref, head_ref, _, w_ref, stay_ref, next_ref, send_ref, held, sems):
     rows = stay_ref.shape[0]
     first = head_ref.shape[0]
-    ends = []
-    for t in TAIL:
-        ends.append((ends[-1] if ends else first) + w_ref.shape[0] // 16 * t)
+    ends = [first + (w_ref.shape[0] - first) // 2, w_ref.shape[0]]
 
     def enter(i):
         start = ends[i - 1] if i else first
@@ -125,7 +122,7 @@
         out_specs=[vmem] * 3,
         scratch_shapes=[
             pltpu.VMEM((f_local - head.shape[0], d_local), bf16),
-            pltpu.SemaphoreType.DMA((len(TAIL),)),
+            pltpu.SemaphoreType.DMA((2,)),
         ],
         out_shape=[
             jax.ShapeDtypeStruct((rows, f_local), bf16),
@@ -221,17 +218,19 @@
     pos = jnp.full((1,), row ^ col, jnp.int32)
     tokens = stack(pos, grads)
     head, mark = fetch(w_down)
-    act_c = swap(act, "col", 1)
-    tokens, act, act_c, act_x, act_y, keep, keep_scaled, mark = lax.optimization_barrier(
-        (tokens, act, act_c, act_x, act_y, keep, keep_scaled, mark)
+    tokens, keep, keep_scaled, mark = lax.optimization_barrier(
+        (tokens, keep, keep_scaled, mark)
     )
 
     tokens_x, act_xy = swap(tokens, "dp", 1), swap(act_x, "col", 2)
+    tokens, act, act_y, act_x, keep, mark = lax.optimization_barrier(
+        (tokens, act, act_y, act_x, keep, mark)
+    )
     stay, onward, send = partial_sums(tokens, keep, head, mark, w_down)
     send, tokens_x, act_xy = lax.optimization_barrier((send, tokens_x, act_xy))
 
     got = swap(send, "col", 1)
-    act_yc, act_xc, act_xyc = [swap(a, "col", 1) for a in (act_y, act_x, act_xy)]
+    act_c, act_yc, act_xc, act_xyc = [swap(a, "col", 1) for a in (act, act_y, act_x, act_xy)]
     mine = stay.astype(f32) + got[:rows].astype(f32)
     theirs = (onward.astype(f32) + got[rows:].astype(f32)).astype(bf16)
     last = swap(theirs, "col", 2)

time: 50.2 us -> 48.1 us (0.958); the launches traced: 49.3 us -> 47.9 us
  waiting for transfers between devices: 6.79 us -> 3.87 us
  starting transfers between devices: 12.8 us -> 14.2 us
    ppermute x13, waiting for transfers between devices: 6.79 us -> 3.87 us  [swap(): return lax.ppermute(x, axis, [(i, i ^ bit) for i in range(n)])]
    ppermute x13, starting transfers between devices: 12.8 us -> 14.2 us  [swap(): return lax.ppermute(x, axis, [(i, i ^ bit) for i in range(n)])]
    pallas_call x1, Pallas kernels: 5.32 us -> 5.93 us  [fetch(): pl.pallas_call(fetch_kernel, in_specs=[anywhere], out_specs=[anywhere, pl...]
    pallas_call x1, Pallas kernels: 8.85 us -> 8.31 us  [partial_sums(): pl.pallas_call(partial_kernel, in_specs=[vmem] * 3 + [pl.BlockSpec(memory...]
  transfers between devices with their start and end apart: 13 -> 13, of which waited for: 8 -> 5; matrix products, arithmetic and copies ran while one was open for 6% -> 6% of each run, Pallas kernels for 50% -> 51%
where the time goes in v3:
time: 48.1 us; the launch traced here: 47.9 us
  Pallas kernels  24.6 us (51%)
  starting transfers between devices  14.2 us (30%)
  other arithmetic  4 us (8%)
  waiting for transfers between devices  3.87 us (8%)
  between operations  0.78 us (2%)
    ppermute x13, starting transfers between devices, swap(): return lax.ppermute(x, axis, [(i, i ^ bit) for i in range(n)])  14.2 us
    pallas_call x1, Pallas kernels, weight_grad(): pl.pallas_call(weight_kernel, in_specs=[vmem] * 11, out_specs=pl.BlockSpe...  10.3 us
    pallas_call x1, Pallas kernels, partial_sums(): pl.pallas_call(partial_kernel, in_specs=[vmem] * 3 + [pl.BlockSpec(memory...  8.31 us
    pallas_call x1, Pallas kernels, fetch(): pl.pallas_call(fetch_kernel, in_specs=[anywhere], out_specs=[anywhere, pl...  5.93 us
    ppermute x13, waiting for transfers between devices, swap(): return lax.ppermute(x, axis, [(i, i ^ bit) for i in range(n)])  3.87 us
    broadcast_in_dim x1, other arithmetic, local(): return (grad_gate[None], grad_up[None], grad_down)  1.51 us
    convert_element_type x1, other arithmetic, activation(): return (gate * jax.nn.sigmoid(gate) * up).astype(bf16)  1.42 us
  transfers between devices with their start and end apart: 13, of which 5 were waited for; matrix products, arithmetic and copies ran while one was open for 6% of the time, Pallas kernels for 51%

profile of v3, /device:TPU:0, one launch (start us, length us, event | category | flops | bytes accessed | tf_op | source)
XLA Modules:
  0.0 47.9 jit_solution(10404785888680585771)
XLA Ops:
  0.6 5.1 %collective-permute-start.2 = (bf16[32,2048]{1,0:T(8,128)(2,1)}, bf16[32,2048]{1,0:T(8,128)(2,1)S(1)}, u32[]{:S(2)}, u32[]{:S(2)}) collective-permute-start(bf16[32,2048]{1,0:T(8,128)(2,1)} %bitcast.28), channel_id=1, source_target_pairs={{0,24},{8,16},{16,8},{24,0},{1,25},{9,17},{17,9},{25,1},{2,26},{10... | collective-permute-start | bytes 393224 | tf_op jit(solution)/shard_map/ppermute | solution.py:22
  5.8 0.6 %collective-permute-start = (bf16[32,2048]{1,0:T(8,128)(2,1)}, bf16[32,2048]{1,0:T(8,128)(2,1)S(1)}, u32[]{:S(2)}, u32[]{:S(2)}) collective-permute-start(bf16[32,2048]{1,0:T(8,128)(2,1)} %bitcast.30), channel_id=1, source_target_pairs={{0,8},{8,0},{16,24},{24,16},{1,9},{9,1},{17,25},{25,17},{2,10},{10... | collective-permute-start | bytes 393224 | tf_op jit(solution)/shard_map/ppermute | solution.py:22
  6.4 1.4 %fusion.refs_0_ = bf16[32,7168]{1,0:T(8,128)(2,1)S(1)} fusion(bf16[1,32,7168]{2,1,0:T(8,128)(2,1)} %param.7, bf16[1,32,7168]{2,1,0:T(8,128)(2,1)} %param.6), kind=kLoop, calls=%fused_computation.6 | loop fusion | flops 1835008 | bytes 1376256 | tf_op jit(solution)/shard_map/convert_element_type | solution.py:195
  7.8 1.7 %collective-permute-start.4 = (bf16[32,7168]{1,0:T(8,128)(2,1)S(1)}, bf16[32,7168]{1,0:T(8,128)(2,1)S(1)}, u32[]{:S(2)}, u32[]{:S(2)}) collective-permute-start(bf16[32,7168]{1,0:T(8,128)(2,1)S(1)} %fusion.refs_0_), channel_id=1, source_target_pairs={{0,1},{1,0},{2,3},{3,2},{4,5},{5,4},{6,7},{7,6},{8,9},{9,8},{10,11... | collective-permute-start | bytes 1376264 | tf_op jit(solution)/shard_map/ppermute | solution.py:22
  9.5 1.5 %collective-permute-start.3 = (bf16[32,7168]{1,0:T(8,128)(2,1)S(1)}, bf16[32,7168]{1,0:T(8,128)(2,1)S(1)}, u32[]{:S(2)}, u32[]{:S(2)}) collective-permute-start(bf16[32,7168]{1,0:T(8,128)(2,1)S(1)} %fusion.refs_0_), channel_id=1, source_target_pairs={{0,4},{2,6},{4,0},{6,2},{1,5},{3,7},{5,1},{7,3},{8,12},{10,14},{12... | collective-permute-start | bytes 1376264 | tf_op jit(solution)/shard_map/ppermute | solution.py:22
  11.0 0.8 %fusion.12 = f32[56,16]{0,1:T(8,128)S(1)} fusion(s32[224,64]{0,1:T(8,128)} %param.9, s32[]{:T(128)S(6)} %select_n.6, s32[]{:T(128)S(6)} %select_n.7), kind=kLoop, calls=%fused_computation.23 | loop fusion | flops 1792 | bytes 7176 | tf_op jit(solution)/shard_map/convert_element_type | solution.py:207
  11.9 0.2 broadcast_in_dim.13
  12.1 0.2 broadcast_multiply_fusion.refs_10_
  12.3 0.1 copy.13
  12.4 5.9 %fetch_weights.1 = (bf16[4096,2048]{1,0:T(8,128)(2,1)S(1)}, f32[8,128]{1,0:T(8,128)S(1)}) custom-call(bf16[7168,2048]{1,0:T(8,128)(2,1)} %w_ref.3), custom_call_target="tpu_custom_call" | custom-call | bytes 16777216 | tf_op jit(solution)/shard_map/fetch_weights/pallas_call | solution.py:65
  18.5 0.6 %collective-permute-start.5 = (bf16[128,2048]{1,0:T(8,128)(2,1)S(1)}, bf16[128,2048]{1,0:T(8,128)(2,1)S(1)}, u32[]{:S(2)}, u32[]{:S(2)}) collective-permute-start(bf16[128,2048]{1,0:T(8,128)(2,1)S(1)} %stack_tokens.1.lhs.refs_8_), channel_id=1, source_target_pairs={{0,1},{1,0},{2,3},{3,2},{4,5},{5,4},{6,7},{7,6},{8,9},{9,8},{10,11... | collective-permute-start | bytes 1572872 | tf_op jit(solution)/shard_map/ppermute | solution.py:22
  19.1 0.5 %collective-permute-done.4.refs_4_ = bf16[32,7168]{1,0:T(8,128)(2,1)S(1)} collective-permute-done((bf16[32,7168]{1,0:T(8,128)(2,1)S(1)}, bf16[32,7168]{1,0:T(8,128)(2,1)S(1)}, u32[]{:S(2)}, u32[]{:S(2)}) %collective-permute-start.4) | collective-permute-done | bytes 458784 | tf_op jit(solution)/shard_map/ppermute | solution.py:22
  19.6 2.1 %collective-permute-start.6 = (bf16[32,7168]{1,0:T(8,128)(2,1)S(1)}, bf16[32,7168]{1,0:T(8,128)(2,1)S(1)}, u32[]{:S(2)}, u32[]{:S(2)}) collective-permute-start(bf16[32,7168]{1,0:T(8,128)(2,1)S(1)} %collective-permute-done.4.refs_4_), channel_id=1, source_target_pairs={{0,4},{2,6},{4,0},{6,2},{1,5},{3,7},{5,1},{7,3},{8,12},{10,14},{12... | collective-permute-start | bytes 1376264 | tf_op jit(solution)/shard_map/ppermute | solution.py:22
  21.7 8.3 %partial_sums.1 = (bf16[32,7168]{1,0:T(8,128)(2,1)S(1)}, bf16[32,7168]{1,0:T(8,128)(2,1)S(1)}, bf16[64,7168]{1,0:T(8,128)(2,1)S(1)}) custom-call(bf16[128,2048]{1,0:T(8,128)(2,1)S(1)} %stack_tokens.1.lhs.refs_8_, f32[56,2048]{1,0:T(8,128)S(1)} %bitcast.27, bf16[4096,2048]{1,0:T(8,128)(2,1)S(1)} %get-tuple-element.27.head_ref, ...), custom_call_target="tpu_custom_call" | custom-call | flops 3758096384 | bytes 29360128 | tf_op jit(solution)/shard_map/partial_sums/pallas_call | solution.py:119
  30.1 0.9 %collective-permute-done.5.refs_9_ = bf16[128,2048]{1,0:T(8,128)(2,1)S(1)} collective-permute-done((bf16[128,2048]{1,0:T(8,128)(2,1)S(1)}, bf16[128,2048]{1,0:T(8,128)(2,1)S(1)}, u32[]{:S(2)}, u32[]{:S(2)}) %collective-permute-start.5) | collective-permute-done | bytes 524320 | tf_op jit(solution)/shard_map/ppermute | solution.py:22
  30.9 0.5 %collective-permute-start.9 = (bf16[32,7168]{1,0:T(8,128)(2,1)S(1)}, bf16[32,7168]{1,0:T(8,128)(2,1)S(1)}, u32[]{:S(2)}, u32[]{:S(2)}) collective-permute-start(bf16[32,7168]{1,0:T(8,128)(2,1)S(1)} %fusion.refs_0_), channel_id=1, source_target_pairs={{0,2},{2,0},{4,6},{6,4},{1,3},{3,1},{5,7},{7,5},{8,10},{10,8},{12,... | collective-permute-start | bytes 1376264 | tf_op jit(solution)/shard_map/ppermute | solution.py:22
  31.4 0.5 %collective-permute-start.11 = (bf16[32,7168]{1,0:T(8,128)(2,1)S(1)}, bf16[32,7168]{1,0:T(8,128)(2,1)S(1)}, u32[]{:S(2)}, u32[]{:S(2)}) collective-permute-start(bf16[32,7168]{1,0:T(8,128)(2,1)S(1)} %collective-permute-done.4.refs_4_), channel_id=1, source_target_pairs={{0,2},{2,0},{4,6},{6,4},{1,3},{3,1},{5,7},{7,5},{8,10},{10,8},{12,... | collective-permute-start | bytes 1376264 | tf_op jit(solution)/shard_map/ppermute | solution.py:22
  32.0 1.4 %collective-permute-done.7 = bf16[64,7168]{1,0:T(8,128)(2,1)S(1)} collective-permute-done((bf16[64,7168]{1,0:T(8,128)(2,1)S(1)}, bf16[64,7168]{1,0:T(8,128)(2,1)S(1)}, u32[]{:S(2)}, u32[]{:S(2)}) %collective-permute-start.7) | collective-permute-done | bytes 917536 | tf_op jit(solution)/shard_map/ppermute | solution.py:22
  33.4 0.1 add_convert_fusion
  33.5 1.5 %collective-permute-start.8 = (bf16[32,7168]{1,0:T(8,128)(2,1)S(1)}, bf16[32,7168]{1,0:T(8,128)(2,1)S(1)}, u32[]{:S(2)}, u32[]{:S(2)}) collective-permute-start(bf16[32,7168]{1,0:T(8,128)(2,1)S(1)} %add_convert_fusion), channel_id=1, source_target_pairs={{0,4},{2,6},{4,0},{6,2},{1,5},{3,7},{5,1},{7,3},{8,12},{10,14},{12... | collective-permute-start | bytes 1376264 | tf_op jit(solution)/shard_map/ppermute | solution.py:22
  35.0 0.4 collective-permute-done.11.refs_6_
  35.4 0.7 %collective-permute-done.12.refs_7_ = bf16[32,7168]{1,0:T(8,128)(2,1)S(1)} collective-permute-done((bf16[32,7168]{1,0:T(8,128)(2,1)S(1)}, bf16[32,7168]{1,0:T(8,128)(2,1)S(1)}, u32[]{:S(2)}, u32[]{:S(2)}) %collective-permute-start.12) | collective-permute-done | bytes 458784 | tf_op jit(solution)/shard_map/ppermute | solution.py:22
  36.0 10.3 %weight_grad.1 = bf16[7168,2048]{1,0:T(8,128)(2,1)} custom-call(bf16[32,7168]{1,0:T(8,128)(2,1)S(1)} %fusion.refs_0_, bf16[32,7168]{1,0:T(8,128)(2,1)S(1)} %collective-permute-done.3.refs_1_, bf16[32,7168]{1,0:T(8,128)(2,1)S(1)} %collective-permute-done.9.refs_2_, bf16[32,7168]{1,0:T(8,128)(2,1)S(1)} %collective-permute-done.10.refs_3_, ...), custom_call_target="tpu_custom_call" | custom-call | flops 7516192768 | bytes 29360128 | tf_op jit(solution)/shard_map/weight_grad/pallas_call | solution.py:176
  46.4 1.5 %fusion.10 = (bf16[1,32,7168]{2,1,0:T(8,128)(2,1)}, bf16[1,32,7168]{2,1,0:T(8,128)(2,1)}) fusion(bf16[1,32,7168]{2,1,0:T(8,128)(2,1)S(1)} %copy-done.1, bf16[32,7168]{1,0:T(8,128)(2,1)S(1)} %collective-permute-done.8, bf16[32,7168]{1,0:T(8,128)(2,1)S(1)} %get-tuple-element.29, bf16[64,7168]{1,0:T(8,128)(2,1)S(1)} %collective-permute-done.7, ...), kind=kLoop, calls=%fused_computation.19 | loop fusion | flops 4587520 | bytes 3211264 | tf_op jit(solution)/shard_map/broadcast_in_dim | solution.py:246
  (20 shorter events, 0.2 us)
Async XLA Ops:
  0.6 17.8 %copy-start = (bf16[1,32,2048]{2,1,0:T(8,128)(2,1)S(1)}, bf16[1,32,2048]{2,1,0:T(8,128)(2,1)}, u32[]{:S(2)}) copy-start(bf16[1,32,2048]{2,1,0:T(8,128)(2,1)} %param.5) | copy-start | bytes 393220
  0.6 17.7 %collective-permute-start.2 = (bf16[32,2048]{1,0:T(8,128)(2,1)}, bf16[32,2048]{1,0:T(8,128)(2,1)S(1)}, u32[]{:S(2)}, u32[]{:S(2)}) collective-permute-start(bf16[32,2048]{1,0:T(8,128)(2,1)} %bitcast.28), channel_id=1, source_target_pairs={{0,24},{8,16},{16,8},{24,0},{1,25},{9,17},{17,9},{25,1},{2,26},{10... | collective-permute-start | bytes 393224 | tf_op jit(solution)/shard_map/ppermute | solution.py:22
  5.8 12.6 %collective-permute-start.1 = (bf16[32,2048]{1,0:T(8,128)(2,1)}, bf16[32,2048]{1,0:T(8,128)(2,1)S(1)}, u32[]{:S(2)}, u32[]{:S(2)}) collective-permute-start(bf16[32,2048]{1,0:T(8,128)(2,1)} %bitcast.29), channel_id=1, source_target_pairs={{0,16},{8,24},{16,0},{24,8},{1,17},{9,25},{17,1},{25,9},{2,18},{10... | collective-permute-start | bytes 393224 | tf_op jit(solution)/shard_map/ppermute | solution.py:22
  5.8 12.6 %collective-permute-start = (bf16[32,2048]{1,0:T(8,128)(2,1)}, bf16[32,2048]{1,0:T(8,128)(2,1)S(1)}, u32[]{:S(2)}, u32[]{:S(2)}) collective-permute-start(bf16[32,2048]{1,0:T(8,128)(2,1)} %bitcast.30), channel_id=1, source_target_pairs={{0,8},{8,0},{16,24},{24,16},{1,9},{9,1},{17,25},{25,17},{2,10},{10... | collective-permute-start | bytes 393224 | tf_op jit(solution)/shard_map/ppermute | solution.py:22
  7.8 11.8 %collective-permute-start.4 = (bf16[32,7168]{1,0:T(8,128)(2,1)S(1)}, bf16[32,7168]{1,0:T(8,128)(2,1)S(1)}, u32[]{:S(2)}, u32[]{:S(2)}) collective-permute-start(bf16[32,7168]{1,0:T(8,128)(2,1)S(1)} %fusion.refs_0_), channel_id=1, source_target_pairs={{0,1},{1,0},{2,3},{3,2},{4,5},{5,4},{6,7},{7,6},{8,9},{9,8},{10,11... | collective-permute-start | bytes 1376264 | tf_op jit(solution)/shard_map/ppermute | solution.py:22
  9.5 12.2 %collective-permute-start.3 = (bf16[32,7168]{1,0:T(8,128)(2,1)S(1)}, bf16[32,7168]{1,0:T(8,128)(2,1)S(1)}, u32[]{:S(2)}, u32[]{:S(2)}) collective-permute-start(bf16[32,7168]{1,0:T(8,128)(2,1)S(1)} %fusion.refs_0_), channel_id=1, source_target_pairs={{0,4},{2,6},{4,0},{6,2},{1,5},{3,7},{5,1},{7,3},{8,12},{10,14},{12... | collective-permute-start | bytes 1376264 | tf_op jit(solution)/shard_map/ppermute | solution.py:22
  18.5 12.5 %collective-permute-start.5 = (bf16[128,2048]{1,0:T(8,128)(2,1)S(1)}, bf16[128,2048]{1,0:T(8,128)(2,1)S(1)}, u32[]{:S(2)}, u32[]{:S(2)}) collective-permute-start(bf16[128,2048]{1,0:T(8,128)(2,1)S(1)} %stack_tokens.1.lhs.refs_8_), channel_id=1, source_target_pairs={{0,1},{1,0},{2,3},{3,2},{4,5},{5,4},{6,7},{7,6},{8,9},{9,8},{10,11... | collective-permute-start | bytes 1572872 | tf_op jit(solution)/shard_map/ppermute | solution.py:22
  19.6 11.3 %collective-permute-start.6 = (bf16[32,7168]{1,0:T(8,128)(2,1)S(1)}, bf16[32,7168]{1,0:T(8,128)(2,1)S(1)}, u32[]{:S(2)}, u32[]{:S(2)}) collective-permute-start(bf16[32,7168]{1,0:T(8,128)(2,1)S(1)} %collective-permute-done.4.refs_4_), channel_id=1, source_target_pairs={{0,4},{2,6},{4,0},{6,2},{1,5},{3,7},{5,1},{7,3},{8,12},{10,14},{12... | collective-permute-start | bytes 1376264 | tf_op jit(solution)/shard_map/ppermute | solution.py:22
  30.0 16.3 %copy-start.1 = (bf16[1,32,7168]{2,1,0:T(8,128)(2,1)S(1)}, bf16[1,32,7168]{2,1,0:T(8,128)(2,1)}, u32[]{:S(2)}) copy-start(bf16[1,32,7168]{2,1,0:T(8,128)(2,1)} %param.6) | copy-start | bytes 1376260
  30.1 16.3 %copy-start.2 = (bf16[1,32,7168]{2,1,0:T(8,128)(2,1)S(1)}, bf16[1,32,7168]{2,1,0:T(8,128)(2,1)}, u32[]{:S(2)}) copy-start(bf16[1,32,7168]{2,1,0:T(8,128)(2,1)} %param.7) | copy-start | bytes 1376260
  30.9 2.5 %collective-permute-start.7 = (bf16[64,7168]{1,0:T(8,128)(2,1)S(1)}, bf16[64,7168]{1,0:T(8,128)(2,1)S(1)}, u32[]{:S(2)}, u32[]{:S(2)}) collective-permute-start(bf16[64,7168]{1,0:T(8,128)(2,1)S(1)} %get-tuple-element.31), channel_id=1, source_target_pairs={{0,2},{2,0},{4,6},{6,4},{1,3},{3,1},{5,7},{7,5},{8,10},{10,8},{12,... | collective-permute-start | bytes 2752520 | tf_op jit(solution)/shard_map/ppermute | solution.py:22
  30.9 4.1 %collective-permute-start.9 = (bf16[32,7168]{1,0:T(8,128)(2,1)S(1)}, bf16[32,7168]{1,0:T(8,128)(2,1)S(1)}, u32[]{:S(2)}, u32[]{:S(2)}) collective-permute-start(bf16[32,7168]{1,0:T(8,128)(2,1)S(1)} %fusion.refs_0_), channel_id=1, source_target_pairs={{0,2},{2,0},{4,6},{6,4},{1,3},{3,1},{5,7},{7,5},{8,10},{10,8},{12,... | collective-permute-start | bytes 1376264 | tf_op jit(solution)/shard_map/ppermute | solution.py:22
  31.4 3.6 %collective-permute-start.10 = (bf16[32,7168]{1,0:T(8,128)(2,1)S(1)}, bf16[32,7168]{1,0:T(8,128)(2,1)S(1)}, u32[]{:S(2)}, u32[]{:S(2)}) collective-permute-start(bf16[32,7168]{1,0:T(8,128)(2,1)S(1)} %collective-permute-done.3.refs_1_), channel_id=1, source_target_pairs={{0,2},{2,0},{4,6},{6,4},{1,3},{3,1},{5,7},{7,5},{8,10},{10,8},{12,... | collective-permute-start | bytes 1376264 | tf_op jit(solution)/shard_map/ppermute | solution.py:22
  31.4 3.9 %collective-permute-start.11 = (bf16[32,7168]{1,0:T(8,128)(2,1)S(1)}, bf16[32,7168]{1,0:T(8,128)(2,1)S(1)}, u32[]{:S(2)}, u32[]{:S(2)}) collective-permute-start(bf16[32,7168]{1,0:T(8,128)(2,1)S(1)} %collective-permute-done.4.refs_4_), channel_id=1, source_target_pairs={{0,2},{2,0},{4,6},{6,4},{1,3},{3,1},{5,7},{7,5},{8,10},{10,8},{12,... | collective-permute-start | bytes 1376264 | tf_op jit(solution)/shard_map/ppermute | solution.py:22
  31.9 4.1 %collective-permute-start.12 = (bf16[32,7168]{1,0:T(8,128)(2,1)S(1)}, bf16[32,7168]{1,0:T(8,128)(2,1)S(1)}, u32[]{:S(2)}, u32[]{:S(2)}) collective-permute-start(bf16[32,7168]{1,0:T(8,128)(2,1)S(1)} %collective-permute-done.6.refs_5_), channel_id=1, source_target_pairs={{0,2},{2,0},{4,6},{6,4},{1,3},{3,1},{5,7},{7,5},{8,10},{10,8},{12,... | collective-permute-start | bytes 1376264 | tf_op jit(solution)/shard_map/ppermute | solution.py:22
  33.5 12.8 %collective-permute-start.8 = (bf16[32,7168]{1,0:T(8,128)(2,1)S(1)}, bf16[32,7168]{1,0:T(8,128)(2,1)S(1)}, u32[]{:S(2)}, u32[]{:S(2)}) collective-permute-start(bf16[32,7168]{1,0:T(8,128)(2,1)S(1)} %add_convert_fusion), channel_id=1, source_target_pairs={{0,4},{2,6},{4,0},{6,2},{1,5},{3,7},{5,1},{7,3},{8,12},{10,14},{12... | collective-permute-start | bytes 1376264 | tf_op jit(solution)/shard_map/ppermute | solution.py:22

commit v4 on v3

--- a/solution.py
+++ b/solution.py
@@ -8,6 +8,7 @@
 BLOCK = 128
 SUB = 256
 IN_TILE = 512
+TAIL_STEPS = 4
 HEAD = 8
 OUT_TILE = 256
 SMALL_VMEM = 4 * 1024 * 1024
@@ -74,7 +75,7 @@
     )(pltpu.with_memory_space_constraint(w, pltpu.HBM))
 
 
-def partial_kernel(lhs, mask_ref, head_ref, _, w_ref, stay_ref, next_ref, send_ref, held, sems):
+def partial_kernel(lhs, mask_ref, head_ref, _, w_ref, stay_ref, next_ref, send_ref, send_next_ref, held, sems):
     rows = stay_ref.shape[0]
     first = head_ref.shape[0]
     ends = [first + (w_ref.shape[0] - first) // 2, w_ref.shape[0]]
@@ -109,7 +110,8 @@
         at = slice(k * SUB, (k + 1) * SUB)
         stay_ref[:, at] = out[:rows]
         next_ref[:, at] = out[rows : 2 * rows]
-        send_ref[:, at] = out[2 * rows :]
+        send_ref[:, at] = out[2 * rows : 3 * rows]
+        send_next_ref[:, at] = out[3 * rows :]
 
 
 def partial_sums(tokens, mask_rows, head, mark, w):
@@ -119,16 +121,15 @@
     return pl.pallas_call(
         partial_kernel,
         in_specs=[vmem] * 3 + [pl.BlockSpec(memory_space=pl.ANY)] * 2,
-        out_specs=[vmem] * 3,
+        out_specs=[vmem] * 4,
         scratch_shapes=[
             pltpu.VMEM((f_local - head.shape[0], d_local), bf16),
             pltpu.SemaphoreType.DMA((2,)),
         ],
         out_shape=[
             jax.ShapeDtypeStruct((rows, f_local), bf16),
-            jax.ShapeDtypeStruct((rows, f_local), bf16),
-            jax.ShapeDtypeStruct((2 * rows, f_local), bf16),
-        ],
+        ]
+        * 4,
         compiler_params=pltpu.CompilerParams(vmem_limit_bytes=PARTIAL_VMEM),
         cost_estimate=pl.CostEstimate(
             flops=2 * 4 * rows * f_local * d_local, bytes_accessed=2 * f_local * d_local, transcendentals=0
@@ -190,6 +191,46 @@
     )(*acts, *tokens, mask_scaled)
 
 
+def tail_kernel(stay, got, last, gate, up, gate_out, up_out, by_gate, by_up, sems):
+    width = stay.shape[1]
+    step = width // TAIL_STEPS
+
+    def leave(i):
+        at = pl.ds(i * step, step)
+        return (
+            pltpu.make_async_copy(by_gate.at[:, at], gate_out.at[:, at], sems.at[0, i]),
+            pltpu.make_async_copy(by_up.at[:, at], up_out.at[:, at], sems.at[1, i]),
+        )
+
+    for i in range(TAIL_STEPS):
+        at = slice(i * step, (i + 1) * step)
+        dact = stay[:, at].astype(f32) + got[:, at].astype(f32) + last[:, at].astype(f32)
+        g, u = gate[:, at].astype(f32), up[:, at].astype(f32)
+        sig = jax.nn.sigmoid(g)
+        by_gate[:, at] = (dact * u * sig * (1.0 + g * (1.0 - sig))).astype(bf16)
+        by_up[:, at] = (dact * g * sig).astype(bf16)
+        for copy in leave(i):
+            copy.start()
+    for i in range(TAIL_STEPS):
+        for copy in leave(i):
+            copy.wait()
+
+
+def tail_grads(stay, got, last, gate, up):
+    vmem, anywhere = pl.BlockSpec(memory_space=pltpu.VMEM), pl.BlockSpec(memory_space=pl.ANY)
+    like = jax.ShapeDtypeStruct(gate.shape, bf16)
+    return pl.pallas_call(
+        tail_kernel,
+        in_specs=[vmem] * 5,
+        out_specs=[anywhere] * 2,
+        out_shape=[like] * 2,
+        scratch_shapes=[pltpu.VMEM(gate.shape, bf16)] * 2
+        + [pltpu.SemaphoreType.DMA((2, TAIL_STEPS))],
+        compiler_params=pltpu.CompilerParams(vmem_limit_bytes=2 * SMALL_VMEM),
+        name="activation_grads",
+    )(stay, got, last, gate, up)
+
+
 def activation(gate, up):
     gate, up = gate.astype(f32), up.astype(f32)
     return (gate * jax.nn.sigmoid(gate) * up).astype(bf16)
@@ -226,23 +267,20 @@
     tokens, act, act_y, act_x, keep, mark = lax.optimization_barrier(
         (tokens, act, act_y, act_x, keep, mark)
     )
-    stay, onward, send = partial_sums(tokens, keep, head, mark, w_down)
-    send, tokens_x, act_xy = lax.optimization_barrier((send, tokens_x, act_xy))
-
+    stay, onward, send, send_next = partial_sums(tokens, keep, head, mark, w_down)
+    send_next, tokens_x, act_xy = lax.optimization_barrier((send_next, tokens_x, act_xy))
+
+    got_next = swap(send_next, "col", 1)
+    act_c, act_yc, act_xc, act_xyc = [swap(a, "col", 1) for a in (act, act_y, act_x, act_xy)]
+    theirs = (onward.astype(f32) + got_next.astype(f32)).astype(bf16)
+    last = swap(theirs, "col", 2)
+    send, act_xyc = lax.optimization_barrier((send, act_xyc))
     got = swap(send, "col", 1)
-    act_c, act_yc, act_xc, act_xyc = [swap(a, "col", 1) for a in (act, act_y, act_x, act_xy)]
-    mine = stay.astype(f32) + got[:rows].astype(f32)
-    theirs = (onward.astype(f32) + got[rows:].astype(f32)).astype(bf16)
-    last = swap(theirs, "col", 2)
 
     acts = [act, act_y, act_c, act_yc, act_x, act_xy, act_xc, act_xyc]
     grad_down = weight_grad(acts, [tokens, tokens_x], keep_scaled)
 
-    dact = mine + last.astype(f32)
-    gate, up = gate.astype(f32), up.astype(f32)
-    sig = jax.nn.sigmoid(gate)
-    grad_gate = (dact * up * sig * (1.0 + gate * (1.0 - sig))).astype(bf16)
-    grad_up = (dact * gate * sig).astype(bf16)
+    grad_gate, grad_up = tail_grads(stay, got, last, gate, up)
     return grad_gate[None], grad_up[None], grad_down
 
 

time: 48.1 us -> 47.6 us (0.990)
  other arithmetic: 4 us -> 2.49 us
  Pallas kernels: 24.6 us -> 25.9 us
  waiting for transfers between devices: 3.87 us -> 3.23 us
    broadcast_in_dim x1 -> x0, other arithmetic: 1.51 us -> none  [local(): return (grad_gate[None], grad_up[None], grad_down)]
    pallas_call x0 -> x1, Pallas kernels: none -> 1.3 us  [tail_grads(): pl.pallas_call(tail_kernel, in_specs=[vmem] * 5, out_specs=[anywhere] * 2...]
    ppermute x13 -> x14, waiting for transfers between devices: 3.87 us -> 3.23 us  [swap(): return lax.ppermute(x, axis, [(i, i ^ bit) for i in range(n)])]
    ppermute x13 -> x14, starting transfers between devices: 14.2 us -> 14.4 us  [swap(): return lax.ppermute(x, axis, [(i, i ^ bit) for i in range(n)])]
  transfers between devices with their start and end apart: 13 -> 14, of which waited for: 5 -> 4; matrix products, arithmetic and copies ran while one was open for 6% -> 6% of each run, Pallas kernels for 51% -> 52%
where the time goes in v4:
time: 47.6 us; the launch traced here: 47.3 us
  Pallas kernels  25.9 us (54%)
  starting transfers between devices  14.4 us (30%)
  waiting for transfers between devices  3.23 us (7%)
  other arithmetic  2.49 us (5%)
  between operations  0.95 us (2%)
    ppermute x14, starting transfers between devices, swap(): return lax.ppermute(x, axis, [(i, i ^ bit) for i in range(n)])  14.4 us
    pallas_call x1, Pallas kernels, weight_grad(): pl.pallas_call(weight_kernel, in_specs=[vmem] * 11, out_specs=pl.BlockSpe...  10.3 us
    pallas_call x1, Pallas kernels, partial_sums(): pl.pallas_call(partial_kernel, in_specs=[vmem] * 3 + [pl.BlockSpec(memory...  8.31 us
    pallas_call x1, Pallas kernels, fetch(): pl.pallas_call(fetch_kernel, in_specs=[anywhere], out_specs=[anywhere, pl...  5.93 us
    ppermute x14, waiting for transfers between devices, swap(): return lax.ppermute(x, axis, [(i, i ^ bit) for i in range(n)])  3.23 us
    convert_element_type x1, other arithmetic, activation(): return (gate * jax.nn.sigmoid(gate) * up).astype(bf16)  1.42 us
    pallas_call x1, Pallas kernels, tail_grads(): pl.pallas_call(tail_kernel, in_specs=[vmem] * 5, out_specs=[anywhere] * 2...  1.3 us
  transfers between devices with their start and end apart: 14, of which 4 were waited for; matrix products, arithmetic and copies ran while one was open for 6% of the time, Pallas kernels for 52%

profile of v4, /device:TPU:0, one launch (start us, length us, event | category | flops | bytes accessed | tf_op | source)
XLA Modules:
  0.0 47.3 jit_solution(15641987469568396446)
XLA Ops:
  0.6 5.1 %collective-permute-start.2 = (bf16[32,2048]{1,0:T(8,128)(2,1)}, bf16[32,2048]{1,0:T(8,128)(2,1)S(1)}, u32[]{:S(2)}, u32[]{:S(2)}) collective-permute-start(bf16[32,2048]{1,0:T(8,128)(2,1)} %bitcast.17), channel_id=1, source_target_pairs={{0,24},{8,16},{16,8},{24,0},{1,25},{9,17},{17,9},{25,1},{2,26},{10... | collective-permute-start | bytes 393224 | tf_op jit(solution)/shard_map/ppermute | solution.py:23
  5.8 0.6 %collective-permute-start = (bf16[32,2048]{1,0:T(8,128)(2,1)}, bf16[32,2048]{1,0:T(8,128)(2,1)S(1)}, u32[]{:S(2)}, u32[]{:S(2)}) collective-permute-start(bf16[32,2048]{1,0:T(8,128)(2,1)} %bitcast.19), channel_id=1, source_target_pairs={{0,8},{8,0},{16,24},{24,16},{1,9},{9,1},{17,25},{25,17},{2,10},{10... | collective-permute-start | bytes 393224 | tf_op jit(solution)/shard_map/ppermute | solution.py:23
  6.4 1.4 %fusion.4.refs_0_ = bf16[32,7168]{1,0:T(8,128)(2,1)S(1)} fusion(bf16[1,32,7168]{2,1,0:T(8,128)(2,1)} %param.7, bf16[1,32,7168]{2,1,0:T(8,128)(2,1)} %param.6), kind=kLoop, calls=%fused_computation.7 | loop fusion | flops 1835008 | bytes 1376256 | tf_op jit(solution)/shard_map/convert_element_type | solution.py:236
  7.8 1.7 %collective-permute-start.4 = (bf16[32,7168]{1,0:T(8,128)(2,1)S(1)}, bf16[32,7168]{1,0:T(8,128)(2,1)S(1)}, u32[]{:S(2)}, u32[]{:S(2)}) collective-permute-start(bf16[32,7168]{1,0:T(8,128)(2,1)S(1)} %fusion.4.refs_0_), channel_id=1, source_target_pairs={{0,1},{1,0},{2,3},{3,2},{4,5},{5,4},{6,7},{7,6},{8,9},{9,8},{10,11... | collective-permute-start | bytes 1376264 | tf_op jit(solution)/shard_map/ppermute | solution.py:23
  9.5 1.5 %collective-permute-start.3 = (bf16[32,7168]{1,0:T(8,128)(2,1)S(1)}, bf16[32,7168]{1,0:T(8,128)(2,1)S(1)}, u32[]{:S(2)}, u32[]{:S(2)}) collective-permute-start(bf16[32,7168]{1,0:T(8,128)(2,1)S(1)} %fusion.4.refs_0_), channel_id=1, source_target_pairs={{0,4},{2,6},{4,0},{6,2},{1,5},{3,7},{5,1},{7,3},{8,12},{10,14},{12... | collective-permute-start | bytes 1376264 | tf_op jit(solution)/shard_map/ppermute | solution.py:23
  11.0 0.8 %fusion.5 = f32[56,16]{0,1:T(8,128)S(1)} fusion(s32[224,64]{0,1:T(8,128)} %param.9, s32[]{:T(128)S(6)} %select_n.6, s32[]{:T(128)S(6)} %select_n.7), kind=kLoop, calls=%fused_computation.11 | loop fusion | flops 1792 | bytes 7176 | tf_op jit(solution)/shard_map/convert_element_type | solution.py:248
  11.9 0.2 broadcast_in_dim.13
  12.1 0.2 broadcast_multiply_fusion.refs_10_
  12.3 0.1 copy.13
  12.4 5.9 %fetch_weights.1 = (bf16[4096,2048]{1,0:T(8,128)(2,1)S(1)}, f32[8,128]{1,0:T(8,128)S(1)}) custom-call(bf16[7168,2048]{1,0:T(8,128)(2,1)} %w_ref.3), custom_call_target="tpu_custom_call" | custom-call | bytes 16777216 | tf_op jit(solution)/shard_map/fetch_weights/pallas_call | solution.py:66
  18.5 0.6 %collective-permute-start.5 = (bf16[128,2048]{1,0:T(8,128)(2,1)S(1)}, bf16[128,2048]{1,0:T(8,128)(2,1)S(1)}, u32[]{:S(2)}, u32[]{:S(2)}) collective-permute-start(bf16[128,2048]{1,0:T(8,128)(2,1)S(1)} %stack_tokens.1.lhs.refs_8_), channel_id=1, source_target_pairs={{0,1},{1,0},{2,3},{3,2},{4,5},{5,4},{6,7},{7,6},{8,9},{9,8},{10,11... | collective-permute-start | bytes 1572872 | tf_op jit(solution)/shard_map/ppermute | solution.py:23
  19.1 0.5 %collective-permute-done.4.refs_4_ = bf16[32,7168]{1,0:T(8,128)(2,1)S(1)} collective-permute-done((bf16[32,7168]{1,0:T(8,128)(2,1)S(1)}, bf16[32,7168]{1,0:T(8,128)(2,1)S(1)}, u32[]{:S(2)}, u32[]{:S(2)}) %collective-permute-start.4) | collective-permute-done | bytes 458784 | tf_op jit(solution)/shard_map/ppermute | solution.py:23
  19.6 2.1 %collective-permute-start.6 = (bf16[32,7168]{1,0:T(8,128)(2,1)S(1)}, bf16[32,7168]{1,0:T(8,128)(2,1)S(1)}, u32[]{:S(2)}, u32[]{:S(2)}) collective-permute-start(bf16[32,7168]{1,0:T(8,128)(2,1)S(1)} %collective-permute-done.4.refs_4_), channel_id=1, source_target_pairs={{0,4},{2,6},{4,0},{6,2},{1,5},{3,7},{5,1},{7,3},{8,12},{10,14},{12... | collective-permute-start | bytes 1376264 | tf_op jit(solution)/shard_map/ppermute | solution.py:23
  21.7 8.3 %partial_sums.1 = (bf16[32,7168]{1,0:T(8,128)(2,1)S(1)}, bf16[32,7168]{1,0:T(8,128)(2,1)S(1)}, bf16[32,7168]{1,0:T(8,128)(2,1)S(1)}, bf16[32,7168]{1,0:T(8,128)(2,1)S(1)}) custom-call(bf16[128,2048]{1,0:T(8,128)(2,1)S(1)} %stack_tokens.1.lhs.refs_8_, f32[56,2048]{1,0:T(8,128)S(1)} %bitcast.14, bf16[4096,2048]{1,0:T(8,128)(2,1)S(1)} %get-tuple-element.32.head_ref, ...), custom_call_target="tpu_custom_call" | custom-call | flops 3758096384 | bytes 29360128 | tf_op jit(solution)/shard_map/partial_sums/pallas_call | solution.py:121
  30.1 0.9 %collective-permute-done.5.refs_9_ = bf16[128,2048]{1,0:T(8,128)(2,1)S(1)} collective-permute-done((bf16[128,2048]{1,0:T(8,128)(2,1)S(1)}, bf16[128,2048]{1,0:T(8,128)(2,1)S(1)}, u32[]{:S(2)}, u32[]{:S(2)}) %collective-permute-start.5) | collective-permute-done | bytes 524320 | tf_op jit(solution)/shard_map/ppermute | solution.py:23
  30.9 0.5 %collective-permute-start.11 = (bf16[32,7168]{1,0:T(8,128)(2,1)S(1)}, bf16[32,7168]{1,0:T(8,128)(2,1)S(1)}, u32[]{:S(2)}, u32[]{:S(2)}) collective-permute-start(bf16[32,7168]{1,0:T(8,128)(2,1)S(1)} %fusion.4.refs_0_), channel_id=1, source_target_pairs={{0,2},{2,0},{4,6},{6,4},{1,3},{3,1},{5,7},{7,5},{8,10},{10,8},{12,... | collective-permute-start | bytes 1376264 | tf_op jit(solution)/shard_map/ppermute | solution.py:23
  31.4 0.5 %collective-permute-start.13 = (bf16[32,7168]{1,0:T(8,128)(2,1)S(1)}, bf16[32,7168]{1,0:T(8,128)(2,1)S(1)}, u32[]{:S(2)}, u32[]{:S(2)}) collective-permute-start(bf16[32,7168]{1,0:T(8,128)(2,1)S(1)} %collective-permute-done.4.refs_4_), channel_id=1, source_target_pairs={{0,2},{2,0},{4,6},{6,4},{1,3},{3,1},{5,7},{7,5},{8,10},{10,8},{12,... | collective-permute-start | bytes 1376264 | tf_op jit(solution)/shard_map/ppermute | solution.py:23
  32.0 0.8 %collective-permute-done.9 = bf16[32,7168]{1,0:T(8,128)(2,1)S(1)} collective-permute-done((bf16[32,7168]{1,0:T(8,128)(2,1)S(1)}, bf16[32,7168]{1,0:T(8,128)(2,1)S(1)}, u32[]{:S(2)}, u32[]{:S(2)}) %collective-permute-start.9) | collective-permute-done | bytes 458784 | tf_op jit(solution)/shard_map/ppermute | solution.py:23
  32.7 0.1 add_convert_fusion
  32.9 1.5 %collective-permute-start.10 = (bf16[32,7168]{1,0:T(8,128)(2,1)S(1)}, bf16[32,7168]{1,0:T(8,128)(2,1)S(1)}, u32[]{:S(2)}, u32[]{:S(2)}) collective-permute-start(bf16[32,7168]{1,0:T(8,128)(2,1)S(1)} %add_convert_fusion), channel_id=1, source_target_pairs={{0,4},{2,6},{4,0},{6,2},{1,5},{3,7},{5,1},{7,3},{8,12},{10,14},{12... | collective-permute-start | bytes 1376264 | tf_op jit(solution)/shard_map/ppermute | solution.py:23
  34.3 1.0 %collective-permute-done.7.refs_7_ = bf16[32,7168]{1,0:T(8,128)(2,1)S(1)} collective-permute-done((bf16[32,7168]{1,0:T(8,128)(2,1)S(1)}, bf16[32,7168]{1,0:T(8,128)(2,1)S(1)}, u32[]{:S(2)}, u32[]{:S(2)}) %collective-permute-start.7) | collective-permute-done | bytes 458784 | tf_op jit(solution)/shard_map/ppermute | solution.py:23
  35.4 0.1 collective-permute-start.8
  35.5 10.3 %weight_grad.1 = bf16[7168,2048]{1,0:T(8,128)(2,1)} custom-call(bf16[32,7168]{1,0:T(8,128)(2,1)S(1)} %fusion.4.refs_0_, bf16[32,7168]{1,0:T(8,128)(2,1)S(1)} %collective-permute-done.3.refs_1_, bf16[32,7168]{1,0:T(8,128)(2,1)S(1)} %collective-permute-done.11.refs_2_, bf16[32,7168]{1,0:T(8,128)(2,1)S(1)} %collective-permute-done.12.refs_3_, ...), custom_call_target="tpu_custom_call" | custom-call | flops 7516192768 | bytes 29360128 | tf_op jit(solution)/shard_map/weight_grad/pallas_call | solution.py:177
  45.9 1.3 %activation_grads.1 = (bf16[32,7168]{1,0:T(8,128)(2,1)}, bf16[32,7168]{1,0:T(8,128)(2,1)}) custom-call(bf16[32,7168]{1,0:T(8,128)(2,1)S(1)} %get-tuple-element.34.stay, bf16[32,7168]{1,0:T(8,128)(2,1)S(1)} %collective-permute-done.8.got, bf16[32,7168]{1,0:T(8,128)(2,1)S(1)} %collective-permute-done.10.last, bf16[32,7168]{1,0:T(8,128)(2,1)S(1)} %bitcast.15, ...), custom_call_target="tpu_custom_call" | custom-call | tf_op jit(solution)/shard_map/activation_grads/pallas_call | solution.py:222
  (22 shorter events, 0.2 us)
Async XLA Ops:
  0.6 17.8 %copy-start.2 = (bf16[1,32,2048]{2,1,0:T(8,128)(2,1)S(1)}, bf16[1,32,2048]{2,1,0:T(8,128)(2,1)}, u32[]{:S(2)}) copy-start(bf16[1,32,2048]{2,1,0:T(8,128)(2,1)} %param.5) | copy-start | bytes 393220
  0.6 17.7 %collective-permute-start.2 = (bf16[32,2048]{1,0:T(8,128)(2,1)}, bf16[32,2048]{1,0:T(8,128)(2,1)S(1)}, u32[]{:S(2)}, u32[]{:S(2)}) collective-permute-start(bf16[32,2048]{1,0:T(8,128)(2,1)} %bitcast.17), channel_id=1, source_target_pairs={{0,24},{8,16},{16,8},{24,0},{1,25},{9,17},{17,9},{25,1},{2,26},{10... | collective-permute-start | bytes 393224 | tf_op jit(solution)/shard_map/ppermute | solution.py:23
  5.8 12.6 %collective-permute-start.1 = (bf16[32,2048]{1,0:T(8,128)(2,1)}, bf16[32,2048]{1,0:T(8,128)(2,1)S(1)}, u32[]{:S(2)}, u32[]{:S(2)}) collective-permute-start(bf16[32,2048]{1,0:T(8,128)(2,1)} %bitcast.18), channel_id=1, source_target_pairs={{0,16},{8,24},{16,0},{24,8},{1,17},{9,25},{17,1},{25,9},{2,18},{10... | collective-permute-start | bytes 393224 | tf_op jit(solution)/shard_map/ppermute | solution.py:23
  5.8 12.6 %collective-permute-start = (bf16[32,2048]{1,0:T(8,128)(2,1)}, bf16[32,2048]{1,0:T(8,128)(2,1)S(1)}, u32[]{:S(2)}, u32[]{:S(2)}) collective-permute-start(bf16[32,2048]{1,0:T(8,128)(2,1)} %bitcast.19), channel_id=1, source_target_pairs={{0,8},{8,0},{16,24},{24,16},{1,9},{9,1},{17,25},{25,17},{2,10},{10... | collective-permute-start | bytes 393224 | tf_op jit(solution)/shard_map/ppermute | solution.py:23
  7.8 11.8 %collective-permute-start.4 = (bf16[32,7168]{1,0:T(8,128)(2,1)S(1)}, bf16[32,7168]{1,0:T(8,128)(2,1)S(1)}, u32[]{:S(2)}, u32[]{:S(2)}) collective-permute-start(bf16[32,7168]{1,0:T(8,128)(2,1)S(1)} %fusion.4.refs_0_), channel_id=1, source_target_pairs={{0,1},{1,0},{2,3},{3,2},{4,5},{5,4},{6,7},{7,6},{8,9},{9,8},{10,11... | collective-permute-start | bytes 1376264 | tf_op jit(solution)/shard_map/ppermute | solution.py:23
  9.5 12.2 %collective-permute-start.3 = (bf16[32,7168]{1,0:T(8,128)(2,1)S(1)}, bf16[32,7168]{1,0:T(8,128)(2,1)S(1)}, u32[]{:S(2)}, u32[]{:S(2)}) collective-permute-start(bf16[32,7168]{1,0:T(8,128)(2,1)S(1)} %fusion.4.refs_0_), channel_id=1, source_target_pairs={{0,4},{2,6},{4,0},{6,2},{1,5},{3,7},{5,1},{7,3},{8,12},{10,14},{12... | collective-permute-start | bytes 1376264 | tf_op jit(solution)/shard_map/ppermute | solution.py:23
  18.5 12.5 %collective-permute-start.5 = (bf16[128,2048]{1,0:T(8,128)(2,1)S(1)}, bf16[128,2048]{1,0:T(8,128)(2,1)S(1)}, u32[]{:S(2)}, u32[]{:S(2)}) collective-permute-start(bf16[128,2048]{1,0:T(8,128)(2,1)S(1)} %stack_tokens.1.lhs.refs_8_), channel_id=1, source_target_pairs={{0,1},{1,0},{2,3},{3,2},{4,5},{5,4},{6,7},{7,6},{8,9},{9,8},{10,11... | collective-permute-start | bytes 1572872 | tf_op jit(solution)/shard_map/ppermute | solution.py:23
  19.6 11.3 %collective-permute-start.6 = (bf16[32,7168]{1,0:T(8,128)(2,1)S(1)}, bf16[32,7168]{1,0:T(8,128)(2,1)S(1)}, u32[]{:S(2)}, u32[]{:S(2)}) collective-permute-start(bf16[32,7168]{1,0:T(8,128)(2,1)S(1)} %collective-permute-done.4.refs_4_), channel_id=1, source_target_pairs={{0,4},{2,6},{4,0},{6,2},{1,5},{3,7},{5,1},{7,3},{8,12},{10,14},{12... | collective-permute-start | bytes 1376264 | tf_op jit(solution)/shard_map/ppermute | solution.py:23
  30.0 15.8 %copy-start = (bf16[1,32,7168]{2,1,0:T(8,128)(2,1)S(1)}, bf16[1,32,7168]{2,1,0:T(8,128)(2,1)}, u32[]{:S(2)}) copy-start(bf16[1,32,7168]{2,1,0:T(8,128)(2,1)} %param.6) | copy-start | bytes 1376260
  30.1 15.8 %copy-start.1 = (bf16[1,32,7168]{2,1,0:T(8,128)(2,1)S(1)}, bf16[1,32,7168]{2,1,0:T(8,128)(2,1)}, u32[]{:S(2)}) copy-start(bf16[1,32,7168]{2,1,0:T(8,128)(2,1)} %param.7) | copy-start | bytes 1376260
  30.9 1.8 %collective-permute-start.9 = (bf16[32,7168]{1,0:T(8,128)(2,1)S(1)}, bf16[32,7168]{1,0:T(8,128)(2,1)S(1)}, u32[]{:S(2)}, u32[]{:S(2)}) collective-permute-start(bf16[32,7168]{1,0:T(8,128)(2,1)S(1)} %get-tuple-element.40), channel_id=1, source_target_pairs={{0,2},{2,0},{4,6},{6,4},{1,3},{3,1},{5,7},{7,5},{8,10},{10,8},{12,... | collective-permute-start | bytes 1376264 | tf_op jit(solution)/shard_map/ppermute | solution.py:23
  30.9 4.6 %collective-permute-start.11 = (bf16[32,7168]{1,0:T(8,128)(2,1)S(1)}, bf16[32,7168]{1,0:T(8,128)(2,1)S(1)}, u32[]{:S(2)}, u32[]{:S(2)}) collective-permute-start(bf16[32,7168]{1,0:T(8,128)(2,1)S(1)} %fusion.4.refs_0_), channel_id=1, source_target_pairs={{0,2},{2,0},{4,6},{6,4},{1,3},{3,1},{5,7},{7,5},{8,10},{10,8},{12,... | collective-permute-start | bytes 1376264 | tf_op jit(solution)/shard_map/ppermute | solution.py:23
  31.4 4.1 %collective-permute-start.12 = (bf16[32,7168]{1,0:T(8,128)(2,1)S(1)}, bf16[32,7168]{1,0:T(8,128)(2,1)S(1)}, u32[]{:S(2)}, u32[]{:S(2)}) collective-permute-start(bf16[32,7168]{1,0:T(8,128)(2,1)S(1)} %collective-permute-done.3.refs_1_), channel_id=1, source_target_pairs={{0,2},{2,0},{4,6},{6,4},{1,3},{3,1},{5,7},{7,5},{8,10},{10,8},{12,... | collective-permute-start | bytes 1376264 | tf_op jit(solution)/shard_map/ppermute | solution.py:23
  31.4 4.1 %collective-permute-start.13 = (bf16[32,7168]{1,0:T(8,128)(2,1)S(1)}, bf16[32,7168]{1,0:T(8,128)(2,1)S(1)}, u32[]{:S(2)}, u32[]{:S(2)}) collective-permute-start(bf16[32,7168]{1,0:T(8,128)(2,1)S(1)} %collective-permute-done.4.refs_4_), channel_id=1, source_target_pairs={{0,2},{2,0},{4,6},{6,4},{1,3},{3,1},{5,7},{7,5},{8,10},{10,8},{12,... | collective-permute-start | bytes 1376264 | tf_op jit(solution)/shard_map/ppermute | solution.py:23
  31.9 3.4 %collective-permute-start.7 = (bf16[32,7168]{1,0:T(8,128)(2,1)S(1)}, bf16[32,7168]{1,0:T(8,128)(2,1)S(1)}, u32[]{:S(2)}, u32[]{:S(2)}) collective-permute-start(bf16[32,7168]{1,0:T(8,128)(2,1)S(1)} %collective-permute-done.6.refs_5_), channel_id=1, source_target_pairs={{0,2},{2,0},{4,6},{6,4},{1,3},{3,1},{5,7},{7,5},{8,10},{10,8},{12,... | collective-permute-start | bytes 1376264 | tf_op jit(solution)/shard_map/ppermute | solution.py:23
  32.9 13.0 %collective-permute-start.10 = (bf16[32,7168]{1,0:T(8,128)(2,1)S(1)}, bf16[32,7168]{1,0:T(8,128)(2,1)S(1)}, u32[]{:S(2)}, u32[]{:S(2)}) collective-permute-start(bf16[32,7168]{1,0:T(8,128)(2,1)S(1)} %add_convert_fusion), channel_id=1, source_target_pairs={{0,4},{2,6},{4,0},{6,2},{1,5},{3,7},{5,1},{7,3},{8,12},{10,14},{12... | collective-permute-start | bytes 1376264 | tf_op jit(solution)/shard_map/ppermute | solution.py:23
  35.4 10.5 %collective-permute-start.8 = (bf16[32,7168]{1,0:T(8,128)(2,1)S(1)}, bf16[32,7168]{1,0:T(8,128)(2,1)S(1)}, u32[]{:S(2)}, u32[]{:S(2)}) collective-permute-start(bf16[32,7168]{1,0:T(8,128)(2,1)S(1)} %get-tuple-element.38), channel_id=1, source_target_pairs={{0,2},{2,0},{4,6},{6,4},{1,3},{3,1},{5,7},{7,5},{8,10},{10,8},{12,... | collective-permute-start | bytes 1376264 | tf_op jit(solution)/shard_map/ppermute | solution.py:23

commit v5 on v4

--- a/solution.py
+++ b/solution.py
@@ -267,11 +267,16 @@
     tokens, act, act_y, act_x, keep, mark = lax.optimization_barrier(
         (tokens, act, act_y, act_x, keep, mark)
     )
+    act_c = swap(act, "col", 1)
     stay, onward, send, send_next = partial_sums(tokens, keep, head, mark, w_down)
-    send_next, tokens_x, act_xy = lax.optimization_barrier((send_next, tokens_x, act_xy))
+    send_next, tokens_x, act_xy, act_c = lax.optimization_barrier(
+        (send_next, tokens_x, act_xy, act_c)
+    )
 
     got_next = swap(send_next, "col", 1)
-    act_c, act_yc, act_xc, act_xyc = [swap(a, "col", 1) for a in (act, act_y, act_x, act_xy)]
+    act_yc = swap(act_y, "col", 1)
+    act_xc = swap(act_x, "col", 1)
+    act_xyc = swap(act_xy, "col", 1)
     theirs = (onward.astype(f32) + got_next.astype(f32)).astype(bf16)
     last = swap(theirs, "col", 2)
     send, act_xyc = lax.optimization_barrier((send, act_xyc))

time: 47.6 us -> 47.4 us (level)
  starting transfers between devices: 14.4 us -> 13.8 us
    ppermute x14, starting transfers between devices: 14.4 us -> 13.8 us  [swap(): return lax.ppermute(x, axis, [(i, i ^ bit) for i in range(n)])]
  transfers between devices with their start and end apart: 14 -> 14, of which waited for: 4 -> 7; matrix products, arithmetic and copies ran while one was open for 6% -> 6% of each run, Pallas kernels for 52% -> 52%
where the time goes in v5:
time: 47.4 us; the launch traced here: 47.2 us
  Pallas kernels  25.9 us (55%)
  starting transfers between devices  13.8 us (29%)
  waiting for transfers between devices  3.61 us (8%)
  other arithmetic  2.49 us (5%)
  between operations  0.93 us (2%)
    ppermute x14, starting transfers between devices, swap(): return lax.ppermute(x, axis, [(i, i ^ bit) for i in range(n)])  13.8 us
    pallas_call x1, Pallas kernels, weight_grad(): pl.pallas_call(weight_kernel, in_specs=[vmem] * 11, out_specs=pl.BlockSpe...  10.3 us
    pallas_call x1, Pallas kernels, partial_sums(): pl.pallas_call(partial_kernel, in_specs=[vmem] * 3 + [pl.BlockSpec(memory...  8.3 us
    pallas_call x1, Pallas kernels, fetch(): pl.pallas_call(fetch_kernel, in_specs=[anywhere], out_specs=[anywhere, pl...  5.93 us
    ppermute x14, waiting for transfers between devices, swap(): return lax.ppermute(x, axis, [(i, i ^ bit) for i in range(n)])  3.61 us
    convert_element_type x1, other arithmetic, activation(): return (gate * jax.nn.sigmoid(gate) * up).astype(bf16)  1.42 us
    pallas_call x1, Pallas kernels, tail_grads(): pl.pallas_call(tail_kernel, in_specs=[vmem] * 5, out_specs=[anywhere] * 2...  1.3 us
  transfers between devices with their start and end apart: 14, of which 7 were waited for; matrix products, arithmetic and copies ran while one was open for 6% of the time, Pallas kernels for 52%

profile of v5, /device:TPU:0, one launch (start us, length us, event | category | flops | bytes accessed | tf_op | source)
XLA Modules:
  0.0 47.2 jit_solution(11275150303540139344)
XLA Ops:
  0.6 5.1 %collective-permute-start.2 = (bf16[32,2048]{1,0:T(8,128)(2,1)}, bf16[32,2048]{1,0:T(8,128)(2,1)S(1)}, u32[]{:S(2)}, u32[]{:S(2)}) collective-permute-start(bf16[32,2048]{1,0:T(8,128)(2,1)} %bitcast.17), channel_id=1, source_target_pairs={{0,24},{8,16},{16,8},{24,0},{1,25},{9,17},{17,9},{25,1},{2,26},{10... | collective-permute-start | bytes 393224 | tf_op jit(solution)/shard_map/ppermute | solution.py:23
  5.8 0.6 %collective-permute-start = (bf16[32,2048]{1,0:T(8,128)(2,1)}, bf16[32,2048]{1,0:T(8,128)(2,1)S(1)}, u32[]{:S(2)}, u32[]{:S(2)}) collective-permute-start(bf16[32,2048]{1,0:T(8,128)(2,1)} %bitcast.19), channel_id=1, source_target_pairs={{0,8},{8,0},{16,24},{24,16},{1,9},{9,1},{17,25},{25,17},{2,10},{10... | collective-permute-start | bytes 393224 | tf_op jit(solution)/shard_map/ppermute | solution.py:23
  6.4 1.4 %fusion.4.refs_0_ = bf16[32,7168]{1,0:T(8,128)(2,1)S(1)} fusion(bf16[1,32,7168]{2,1,0:T(8,128)(2,1)} %param.7, bf16[1,32,7168]{2,1,0:T(8,128)(2,1)} %param.6), kind=kLoop, calls=%fused_computation.7 | loop fusion | flops 1835008 | bytes 1376256 | tf_op jit(solution)/shard_map/convert_element_type | solution.py:236
  7.8 1.7 %collective-permute-start.4 = (bf16[32,7168]{1,0:T(8,128)(2,1)S(1)}, bf16[32,7168]{1,0:T(8,128)(2,1)S(1)}, u32[]{:S(2)}, u32[]{:S(2)}) collective-permute-start(bf16[32,7168]{1,0:T(8,128)(2,1)S(1)} %fusion.4.refs_0_), channel_id=1, source_target_pairs={{0,1},{1,0},{2,3},{3,2},{4,5},{5,4},{6,7},{7,6},{8,9},{9,8},{10,11... | collective-permute-start | bytes 1376264 | tf_op jit(solution)/shard_map/ppermute | solution.py:23
  9.5 1.5 %collective-permute-start.3 = (bf16[32,7168]{1,0:T(8,128)(2,1)S(1)}, bf16[32,7168]{1,0:T(8,128)(2,1)S(1)}, u32[]{:S(2)}, u32[]{:S(2)}) collective-permute-start(bf16[32,7168]{1,0:T(8,128)(2,1)S(1)} %fusion.4.refs_0_), channel_id=1, source_target_pairs={{0,4},{2,6},{4,0},{6,2},{1,5},{3,7},{5,1},{7,3},{8,12},{10,14},{12... | collective-permute-start | bytes 1376264 | tf_op jit(solution)/shard_map/ppermute | solution.py:23
  11.0 0.8 %fusion.5 = f32[56,16]{0,1:T(8,128)S(1)} fusion(s32[224,64]{0,1:T(8,128)} %param.9, s32[]{:T(128)S(6)} %select_n.6, s32[]{:T(128)S(6)} %select_n.7), kind=kLoop, calls=%fused_computation.11 | loop fusion | flops 1792 | bytes 7176 | tf_op jit(solution)/shard_map/convert_element_type | solution.py:248
  11.9 0.2 broadcast_in_dim.13
  12.1 0.2 broadcast_multiply_fusion.refs_10_
  12.4 5.9 %fetch_weights.1 = (bf16[4096,2048]{1,0:T(8,128)(2,1)S(1)}, f32[8,128]{1,0:T(8,128)S(1)}) custom-call(bf16[7168,2048]{1,0:T(8,128)(2,1)} %w_ref.3), custom_call_target="tpu_custom_call" | custom-call | bytes 16777216 | tf_op jit(solution)/shard_map/fetch_weights/pallas_call | solution.py:66
  18.5 0.6 %collective-permute-start.5 = (bf16[128,2048]{1,0:T(8,128)(2,1)S(1)}, bf16[128,2048]{1,0:T(8,128)(2,1)S(1)}, u32[]{:S(2)}, u32[]{:S(2)}) collective-permute-start(bf16[128,2048]{1,0:T(8,128)(2,1)S(1)} %stack_tokens.1.lhs.refs_8_), channel_id=1, source_target_pairs={{0,1},{1,0},{2,3},{3,2},{4,5},{5,4},{6,7},{7,6},{8,9},{9,8},{10,11... | collective-permute-start | bytes 1572872 | tf_op jit(solution)/shard_map/ppermute | solution.py:23
  19.1 0.5 %collective-permute-done.4.refs_4_ = bf16[32,7168]{1,0:T(8,128)(2,1)S(1)} collective-permute-done((bf16[32,7168]{1,0:T(8,128)(2,1)S(1)}, bf16[32,7168]{1,0:T(8,128)(2,1)S(1)}, u32[]{:S(2)}, u32[]{:S(2)}) %collective-permute-start.4) | collective-permute-done | bytes 458784 | tf_op jit(solution)/shard_map/ppermute | solution.py:23
  19.6 1.2 %collective-permute-done.3.refs_1_ = bf16[32,7168]{1,0:T(8,128)(2,1)S(1)} collective-permute-done((bf16[32,7168]{1,0:T(8,128)(2,1)S(1)}, bf16[32,7168]{1,0:T(8,128)(2,1)S(1)}, u32[]{:S(2)}, u32[]{:S(2)}) %collective-permute-start.3) | collective-permute-done | bytes 458784 | tf_op jit(solution)/shard_map/ppermute | solution.py:23
  20.8 1.5 %collective-permute-start.6 = (bf16[32,7168]{1,0:T(8,128)(2,1)S(1)}, bf16[32,7168]{1,0:T(8,128)(2,1)S(1)}, u32[]{:S(2)}, u32[]{:S(2)}) collective-permute-start(bf16[32,7168]{1,0:T(8,128)(2,1)S(1)} %collective-permute-done.4.refs_4_), channel_id=1, source_target_pairs={{0,4},{2,6},{4,0},{6,2},{1,5},{3,7},{5,1},{7,3},{8,12},{10,14},{12... | collective-permute-start | bytes 1376264 | tf_op jit(solution)/shard_map/ppermute | solution.py:23
  22.3 8.3 %partial_sums.1 = (bf16[32,7168]{1,0:T(8,128)(2,1)S(1)}, bf16[32,7168]{1,0:T(8,128)(2,1)S(1)}, bf16[32,7168]{1,0:T(8,128)(2,1)S(1)}, bf16[32,7168]{1,0:T(8,128)(2,1)S(1)}) custom-call(bf16[128,2048]{1,0:T(8,128)(2,1)S(1)} %stack_tokens.1.lhs.refs_8_, f32[56,2048]{1,0:T(8,128)S(1)} %bitcast.14, bf16[4096,2048]{1,0:T(8,128)(2,1)S(1)} %get-tuple-element.33.head_ref, ...), custom_call_target="tpu_custom_call" | custom-call | flops 3758096384 | bytes 29360128 | tf_op jit(solution)/shard_map/partial_sums/pallas_call | solution.py:121
  30.7 0.3 collective-permute-done.5.refs_9_
  30.9 0.2 collective-permute-done.6.refs_5_
  31.3 0.4 collective-permute-start.12
  31.8 0.4 collective-permute-start.8
  32.2 0.8 %collective-permute-done.10 = bf16[32,7168]{1,0:T(8,128)(2,1)S(1)} collective-permute-done((bf16[32,7168]{1,0:T(8,128)(2,1)S(1)}, bf16[32,7168]{1,0:T(8,128)(2,1)S(1)}, u32[]{:S(2)}, u32[]{:S(2)}) %collective-permute-start.10) | collective-permute-done | bytes 458784 | tf_op jit(solution)/shard_map/ppermute | solution.py:23
  33.1 1.6 %collective-permute-start.11 = (bf16[32,7168]{1,0:T(8,128)(2,1)S(1)}, bf16[32,7168]{1,0:T(8,128)(2,1)S(1)}, u32[]{:S(2)}, u32[]{:S(2)}) collective-permute-start(bf16[32,7168]{1,0:T(8,128)(2,1)S(1)} %add_convert_fusion), channel_id=1, source_target_pairs={{0,4},{2,6},{4,0},{6,2},{1,5},{3,7},{5,1},{7,3},{8,12},{10,14},{12... | collective-permute-start | bytes 1376264 | tf_op jit(solution)/shard_map/ppermute | solution.py:23
  34.7 0.3 collective-permute-done.8.refs_7_
  35.1 10.3 %weight_grad.1 = bf16[7168,2048]{1,0:T(8,128)(2,1)} custom-call(bf16[32,7168]{1,0:T(8,128)(2,1)S(1)} %fusion.4.refs_0_, bf16[32,7168]{1,0:T(8,128)(2,1)S(1)} %collective-permute-done.3.refs_1_, bf16[32,7168]{1,0:T(8,128)(2,1)S(1)} %collective-permute-done.7.refs_2_, bf16[32,7168]{1,0:T(8,128)(2,1)S(1)} %collective-permute-done.12.refs_3_, ...), custom_call_target="tpu_custom_call" | custom-call | flops 7516192768 | bytes 29360128 | tf_op jit(solution)/shard_map/weight_grad/pallas_call | solution.py:177
  45.4 0.3 collective-permute-done.11.last
  45.7 1.3 %activation_grads.1 = (bf16[32,7168]{1,0:T(8,128)(2,1)}, bf16[32,7168]{1,0:T(8,128)(2,1)}) custom-call(bf16[32,7168]{1,0:T(8,128)(2,1)S(1)} %get-tuple-element.35.stay, bf16[32,7168]{1,0:T(8,128)(2,1)S(1)} %collective-permute-done.9.got, bf16[32,7168]{1,0:T(8,128)(2,1)S(1)} %collective-permute-done.11.last, bf16[32,7168]{1,0:T(8,128)(2,1)S(1)} %bitcast.15, ...), custom_call_target="tpu_custom_call" | custom-call | tf_op jit(solution)/shard_map/activation_grads/pallas_call | solution.py:222
  (22 shorter events, 0.8 us)
Async XLA Ops:
  0.6 17.8 %copy-start.2 = (bf16[1,32,2048]{2,1,0:T(8,128)(2,1)S(1)}, bf16[1,32,2048]{2,1,0:T(8,128)(2,1)}, u32[]{:S(2)}) copy-start(bf16[1,32,2048]{2,1,0:T(8,128)(2,1)} %param.5) | copy-start | bytes 393220
  0.6 17.7 %collective-permute-start.2 = (bf16[32,2048]{1,0:T(8,128)(2,1)}, bf16[32,2048]{1,0:T(8,128)(2,1)S(1)}, u32[]{:S(2)}, u32[]{:S(2)}) collective-permute-start(bf16[32,2048]{1,0:T(8,128)(2,1)} %bitcast.17), channel_id=1, source_target_pairs={{0,24},{8,16},{16,8},{24,0},{1,25},{9,17},{17,9},{25,1},{2,26},{10... | collective-permute-start | bytes 393224 | tf_op jit(solution)/shard_map/ppermute | solution.py:23
  5.8 12.6 %collective-permute-start.1 = (bf16[32,2048]{1,0:T(8,128)(2,1)}, bf16[32,2048]{1,0:T(8,128)(2,1)S(1)}, u32[]{:S(2)}, u32[]{:S(2)}) collective-permute-start(bf16[32,2048]{1,0:T(8,128)(2,1)} %bitcast.18), channel_id=1, source_target_pairs={{0,16},{8,24},{16,0},{24,8},{1,17},{9,25},{17,1},{25,9},{2,18},{10... | collective-permute-start | bytes 393224 | tf_op jit(solution)/shard_map/ppermute | solution.py:23
  5.8 12.6 %collective-permute-start = (bf16[32,2048]{1,0:T(8,128)(2,1)}, bf16[32,2048]{1,0:T(8,128)(2,1)S(1)}, u32[]{:S(2)}, u32[]{:S(2)}) collective-permute-start(bf16[32,2048]{1,0:T(8,128)(2,1)} %bitcast.19), channel_id=1, source_target_pairs={{0,8},{8,0},{16,24},{24,16},{1,9},{9,1},{17,25},{25,17},{2,10},{10... | collective-permute-start | bytes 393224 | tf_op jit(solution)/shard_map/ppermute | solution.py:23
  7.8 11.8 %collective-permute-start.4 = (bf16[32,7168]{1,0:T(8,128)(2,1)S(1)}, bf16[32,7168]{1,0:T(8,128)(2,1)S(1)}, u32[]{:S(2)}, u32[]{:S(2)}) collective-permute-start(bf16[32,7168]{1,0:T(8,128)(2,1)S(1)} %fusion.4.refs_0_), channel_id=1, source_target_pairs={{0,1},{1,0},{2,3},{3,2},{4,5},{5,4},{6,7},{7,6},{8,9},{9,8},{10,11... | collective-permute-start | bytes 1376264 | tf_op jit(solution)/shard_map/ppermute | solution.py:23
  9.5 11.3 %collective-permute-start.3 = (bf16[32,7168]{1,0:T(8,128)(2,1)S(1)}, bf16[32,7168]{1,0:T(8,128)(2,1)S(1)}, u32[]{:S(2)}, u32[]{:S(2)}) collective-permute-start(bf16[32,7168]{1,0:T(8,128)(2,1)S(1)} %fusion.4.refs_0_), channel_id=1, source_target_pairs={{0,4},{2,6},{4,0},{6,2},{1,5},{3,7},{5,1},{7,3},{8,12},{10,14},{12... | collective-permute-start | bytes 1376264 | tf_op jit(solution)/shard_map/ppermute | solution.py:23
  18.5 12.5 %collective-permute-start.5 = (bf16[128,2048]{1,0:T(8,128)(2,1)S(1)}, bf16[128,2048]{1,0:T(8,128)(2,1)S(1)}, u32[]{:S(2)}, u32[]{:S(2)}) collective-permute-start(bf16[128,2048]{1,0:T(8,128)(2,1)S(1)} %stack_tokens.1.lhs.refs_8_), channel_id=1, source_target_pairs={{0,1},{1,0},{2,3},{3,2},{4,5},{5,4},{6,7},{7,6},{8,9},{9,8},{10,11... | collective-permute-start | bytes 1572872 | tf_op jit(solution)/shard_map/ppermute | solution.py:23
  20.8 10.4 %collective-permute-start.6 = (bf16[32,7168]{1,0:T(8,128)(2,1)S(1)}, bf16[32,7168]{1,0:T(8,128)(2,1)S(1)}, u32[]{:S(2)}, u32[]{:S(2)}) collective-permute-start(bf16[32,7168]{1,0:T(8,128)(2,1)S(1)} %collective-permute-done.4.refs_4_), channel_id=1, source_target_pairs={{0,4},{2,6},{4,0},{6,2},{1,5},{3,7},{5,1},{7,3},{8,12},{10,14},{12... | collective-permute-start | bytes 1376264 | tf_op jit(solution)/shard_map/ppermute | solution.py:23
  22.3 8.8 %collective-permute-start.7 = (bf16[32,7168]{1,0:T(8,128)(2,1)S(1)}, bf16[32,7168]{1,0:T(8,128)(2,1)S(1)}, u32[]{:S(2)}, u32[]{:S(2)}) collective-permute-start(bf16[32,7168]{1,0:T(8,128)(2,1)S(1)} %fusion.4.refs_0_), channel_id=1, source_target_pairs={{0,2},{2,0},{4,6},{6,4},{1,3},{3,1},{5,7},{7,5},{8,10},{10,8},{12,... | collective-permute-start | bytes 1376264 | tf_op jit(solution)/shard_map/ppermute | solution.py:23
  30.6 15.1 %copy-start = (bf16[1,32,7168]{2,1,0:T(8,128)(2,1)S(1)}, bf16[1,32,7168]{2,1,0:T(8,128)(2,1)}, u32[]{:S(2)}) copy-start(bf16[1,32,7168]{2,1,0:T(8,128)(2,1)} %param.6) | copy-start | bytes 1376260
  30.6 15.1 %copy-start.1 = (bf16[1,32,7168]{2,1,0:T(8,128)(2,1)S(1)}, bf16[1,32,7168]{2,1,0:T(8,128)(2,1)}, u32[]{:S(2)}) copy-start(bf16[1,32,7168]{2,1,0:T(8,128)(2,1)} %param.7) | copy-start | bytes 1376260
  31.2 1.8 %collective-permute-start.10 = (bf16[32,7168]{1,0:T(8,128)(2,1)S(1)}, bf16[32,7168]{1,0:T(8,128)(2,1)S(1)}, u32[]{:S(2)}, u32[]{:S(2)}) collective-permute-start(bf16[32,7168]{1,0:T(8,128)(2,1)S(1)} %get-tuple-element.42), channel_id=1, source_target_pairs={{0,2},{2,0},{4,6},{6,4},{1,3},{3,1},{5,7},{7,5},{8,10},{10,8},{12,... | collective-permute-start | bytes 1376264 | tf_op jit(solution)/shard_map/ppermute | solution.py:23
  31.3 3.8 %collective-permute-start.12 = (bf16[32,7168]{1,0:T(8,128)(2,1)S(1)}, bf16[32,7168]{1,0:T(8,128)(2,1)S(1)}, u32[]{:S(2)}, u32[]{:S(2)}) collective-permute-start(bf16[32,7168]{1,0:T(8,128)(2,1)S(1)} %collective-permute-done.3.refs_1_), channel_id=1, source_target_pairs={{0,2},{2,0},{4,6},{6,4},{1,3},{3,1},{5,7},{7,5},{8,10},{10,8},{12,... | collective-permute-start | bytes 1376264 | tf_op jit(solution)/shard_map/ppermute | solution.py:23
  31.7 3.4 %collective-permute-start.13 = (bf16[32,7168]{1,0:T(8,128)(2,1)S(1)}, bf16[32,7168]{1,0:T(8,128)(2,1)S(1)}, u32[]{:S(2)}, u32[]{:S(2)}) collective-permute-start(bf16[32,7168]{1,0:T(8,128)(2,1)S(1)} %collective-permute-done.4.refs_4_), channel_id=1, source_target_pairs={{0,2},{2,0},{4,6},{6,4},{1,3},{3,1},{5,7},{7,5},{8,10},{10,8},{12,... | collective-permute-start | bytes 1376264 | tf_op jit(solution)/shard_map/ppermute | solution.py:23
  31.8 3.2 %collective-permute-start.8 = (bf16[32,7168]{1,0:T(8,128)(2,1)S(1)}, bf16[32,7168]{1,0:T(8,128)(2,1)S(1)}, u32[]{:S(2)}, u32[]{:S(2)}) collective-permute-start(bf16[32,7168]{1,0:T(8,128)(2,1)S(1)} %collective-permute-done.6.refs_5_), channel_id=1, source_target_pairs={{0,2},{2,0},{4,6},{6,4},{1,3},{3,1},{5,7},{7,5},{8,10},{10,8},{12,... | collective-permute-start | bytes 1376264 | tf_op jit(solution)/shard_map/ppermute | solution.py:23
  33.1 12.6 %collective-permute-start.11 = (bf16[32,7168]{1,0:T(8,128)(2,1)S(1)}, bf16[32,7168]{1,0:T(8,128)(2,1)S(1)}, u32[]{:S(2)}, u32[]{:S(2)}) collective-permute-start(bf16[32,7168]{1,0:T(8,128)(2,1)S(1)} %add_convert_fusion), channel_id=1, source_target_pairs={{0,4},{2,6},{4,0},{6,2},{1,5},{3,7},{5,1},{7,3},{8,12},{10,14},{12... | collective-permute-start | bytes 1376264 | tf_op jit(solution)/shard_map/ppermute | solution.py:23
  34.9 10.8 %collective-permute-start.9 = (bf16[32,7168]{1,0:T(8,128)(2,1)S(1)}, bf16[32,7168]{1,0:T(8,128)(2,1)S(1)}, u32[]{:S(2)}, u32[]{:S(2)}) collective-permute-start(bf16[32,7168]{1,0:T(8,128)(2,1)S(1)} %get-tuple-element.40), channel_id=1, source_target_pairs={{0,2},{2,0},{4,6},{6,4},{1,3},{3,1},{5,7},{7,5},{8,10},{10,8},{12,... | collective-permute-start | bytes 1376264 | tf_op jit(solution)/shard_map/ppermute | solution.py:23
